TPU v7x, 128 devices: a whole 4x4x4 slice. The times are simulated.
128 devices in a mesh: seq: 32 (over x, z, core), dp: 4 (over y).
Axes of the slice: x: 4, y: 4, z: 4, core: 2. Of those that a mesh axis runs over, the one named last changes fastest.
Arguments:
- tokens: bfloat16 [4, 6144, 640], P('dp', 'seq'), may hold values from -6 to 6
- lengths: int32 [4, 2], P('dp'), may hold values from 2048 to 4096, as said below
- w_query: bfloat16 [640, 1024], replicated, may hold values from -0.25 to 0.25
- w_key: bfloat16 [640, 256], replicated, may hold values from -0.25 to 0.25
- w_value: bfloat16 [640, 256], replicated, may hold values from -0.25 to 0.25
- w_output: bfloat16 [1024, 640], replicated, may hold values from -1.5 to 1.5
- w_gate: bfloat16 [640, 2048], replicated, may hold values from -0.25 to 0.25
- w_up: bfloat16 [640, 2048], replicated, may hold values from -0.25 to 0.25
- w_down: bfloat16 [2048, 640], replicated, may hold values from -0.125 to 0.125
- gain_attn: float32 [640], replicated, may hold values from 0.1 to 1.9
- gain_mlp: float32 [640], replicated, may hold values from 0.1 to 1.9
- out_grad: bfloat16 [4, 6144, 640], P('dp', 'seq'), may hold values from -6 to 6
Outputs:
- block_out: bfloat16 [4, 6144, 640], P('dp', 'seq')
- shared_kv: bfloat16 [4, 6144, 512], P('dp', 'seq')
- input_grad: float32 [4, 6144, 640], P('dp', 'seq')
- grad_query: float32 [640, 1024], replicated
- grad_key: float32 [640, 256], replicated
- grad_value: float32 [640, 256], replicated
- grad_proj: float32 [1024, 640], replicated
- grad_gate: float32 [640, 2048], replicated
- grad_up: float32 [640, 2048], replicated
- grad_down: float32 [2048, 640], replicated
- grad_gain_attn: float32 [640], replicated
- grad_gain_mlp: float32 [640], replicated
Inputs may be any that keep to these rules, and one draw needn't show every extreme that they name: `lengths`: in each row, 1 entries are 2048 and 1 are 4096, in an order drawn for each row.
All inputs are finite; a program needn't handle non-finite values.
Results may differ from a plain program's by a relative error of at most 0.015.
Values may be sent and summed in bfloat16 or wider, within the bound.
No kernel may reach another device: no remote copies, remote signals or barrier semaphores. Data moves between devices by JAX's collectives and lax.ppermute only.
A program may use at most 128 MiB of HBM per device.

v0:
```python
import jax
import jax.numpy as jnp
import numpy as np
from jax import lax
from jax.experimental import pallas as pl
from jax.experimental.pallas import tpu as pltpu
from jax.sharding import Mesh, PartitionSpec as P

WINDOW = 1024
SHORT_LEN = 2048
D = 640
HEADS = 4
HD = 256
HALF = 128
FF = 2048
TOK = 192
SHORT = 64
LONG = 128
CHIPS = 16
NEAR = 4
FAR = 8
SIDE = (NEAR + 1) * TOK + (FAR - NEAR) * SHORT
GROUPS = SIDE // SHORT
WINDOW_PARTS = ((0, NEAR, FAR), (1, 5), (2, 6), (3, 7))
KNOWN = 2 * TOK + SHORT
ROUND = TOK + SHORT
KEYS_SHORT = 2 * (FAR + 1) * SHORT
KEYS_LONG = 2 * (NEAR + 1) * LONG
KEYS = KEYS_SHORT + KEYS_LONG
FF_CHUNK = 512
NORM_ROWS = 304

epsilon = 1e-06
theta_base = 10000.0
masked_score = -1e30

SEQ = ("x", "z", "core")
CHIP = ("x", "z")
ALL = ("x", "z", "core", "dp")
HALF_FF = FF // 2
AT_GATE, AT_UP, AT_MIXED, AT_NORMED, AT_OUT, AT_BRANCH = 1024, 2048, 3072, 3584, 4224, 4864
ACTS = 5504
A_GATE, A_UP, A_DOWN, A_PROJ, A_GAIN, A_ROWS = 0, 5120, 10240, 15360, 17920, 18432
B_QUERY, B_KV, B_GAIN, B_ROWS = 0, 2560, 3840, 4096
DP = 4
A_DP = 7168
A_XZ = A_ROWS - A_DP
A_DP_PIECE, B_PIECE, A_XZ_PIECE = A_DP // DP, B_ROWS // DP, A_XZ // CHIPS
A_DP_BLOCK, B_BLOCK, A_XZ_BLOCK = A_DP_PIECE // CHIPS, B_PIECE // CHIPS, A_XZ_PIECE // DP
BLOCK = A_DP_BLOCK + B_BLOCK + A_XZ_BLOCK
XZ_FIRST = 192
JOINED = XZ_FIRST - A_DP_BLOCK - B_BLOCK
DP_FIRST = A_XZ_BLOCK - JOINED

bf16 = jnp.bfloat16
f32 = jnp.float32


def mm(left, right):
    return jnp.dot(left, right, preferred_element_type=f32)


def mm_tn(left, right):
    return lax.dot_general(left, right, (((0,), (0,)), ((), ())), preferred_element_type=f32)


def mm_nt(left, right):
    return lax.dot_general(left, right, (((1,), (1,)), ((), ())), preferred_element_type=f32)


def window_groups():
    groups = []
    for pieces in WINDOW_PARTS:
        for behind in pieces:
            groups.append((behind, "short", 0))
            if behind <= NEAR:
                groups += [(behind, "long", 0), (behind, "long", 1)]
    return groups


def key_row(side, group):
    behind, kind, part = group
    if kind == "short":
        return side * (KEYS_SHORT // 2) + behind * SHORT
    return KEYS_SHORT + side * (KEYS_LONG // 2) + behind * LONG + part * SHORT


def mask_bias(kind, chip, core):
    rows, width, first_key = (SHORT, KEYS_SHORT, 0) if kind == "short" else (LONG, KEYS_LONG, 0)
    half = width // 2
    column = lax.broadcasted_iota(jnp.int32, (1, width), 1)
    other = (column >= half).astype(jnp.int32)
    inner = column - other * half
    shift = 6 if kind == "short" else 7
    behind = lax.shift_right_logical(inner, shift)
    rest = inner & (rows - 1)
    key_core = core + other * (1 - 2 * core)
    key_position = (2 * (chip - behind) + key_core) * rows + rest
    query_position = (2 * chip + core) * rows + lax.broadcasted_iota(jnp.int32, (rows, 1), 0)
    distance = query_position - key_position
    allowed = (key_position >= 0) & (distance >= 0) & (distance < WINDOW)
    return jnp.where(allowed, 0.0, masked_score).astype(f32)


def group_tables(tables, chip, core, side, group):
    behind, kind, part = group
    piece = 2 * (chip - behind) + (core if side == 0 else 1 - core)
    at = jnp.maximum(piece if kind == "short" else 2 * piece + part, 0)
    cb, sb = tables[0, pl.ds(at, 1), :], tables[1, pl.ds(at, 1), :]
    cr, sr = tables[2], tables[3]
    return cb * cr - sb * sr, sb * cr + cb * sr


def rotary_tables():
    frequency = theta_base ** (-(np.arange(HALF) * 2.0 / HD))
    far = np.arange(SHORT)[:, None] * SHORT * frequency[None, :]
    near = np.arange(SHORT)[:, None] * frequency[None, :]
    return np.stack([np.cos(far), np.sin(far), np.cos(near), np.sin(near)]).astype(np.float32)


def place():
    return lax.axis_index("x") * 4 + lax.axis_index("z"), lax.axis_index("core")


def starts(lengths):
    short_first = (lengths[0, 0] == SHORT_LEN).astype(jnp.int32)
    return pl.multiple_of((1 - short_first) * LONG, SHORT), pl.multiple_of(short_first * SHORT, SHORT)


KINDS = (
    ("short", SHORT, 0, KEYS_SHORT, 0, 0),
    ("long", LONG, KEYS_SHORT, KEYS_LONG, HEADS * SHORT, SHORT),
)


def copies_of(pairs, sems, first=0):
    copies = [
        pltpu.make_async_copy(source, target, sems.at[first + number])
        for number, (source, target) in enumerate(pairs)
    ]
    for copy in copies:
        copy.start()
    return copies


class Stores:
    def __init__(self, sems):
        self.sems, self.copies = sems, []

    def start(self, source, target):
        self.copies += copies_of([(source, target)], self.sems, len(self.copies))

    def wait(self):
        for copy in self.copies:
            copy.wait()


def forward_kernel(
    lengths, tables, ga, gm, w0_h, w1_h, w2_h, w3_h, w4_h, w5_h, w6_h, w7_h, og_h, wq_h, wk_h, wv_h, wo_h, wg_h, wu_h, wd_h,
    ggain_o, q_h, k_h, v_h, gmix_h, norm_h, gres_h, bo_h, skv_h, keep_h, send_h,
    win, og, wq, wk, wv, wo, wg, wu, wd, norm, q, k, v, kv, scores_all, probs_all, mixed, gmix, gres,
    bo, skv, acts, bias_s, bias_l, out_sum, grad_sum, win_sem, sems, out_sem,
):
    chip, core = place()
    short_at, long_at = starts(lengths)
    window_loads = []
    for side, (known, *rounds) in enumerate(((w0_h, w1_h, w2_h, w3_h), (w4_h, w5_h, w6_h, w7_h))):
        base = side * SIDE
        at = base
        for source, pieces in zip((known, *rounds), WINDOW_PARTS):
            first = 0
            for behind in pieces:
                if behind <= NEAR:
                    window_loads += [
                        (source.at[pl.ds(first + short_at, SHORT)], win.at[pl.ds(at, SHORT)]),
                        (source.at[pl.ds(first + long_at, LONG)], win.at[pl.ds(at + SHORT, LONG)]),
                    ]
                    first, at = first + TOK, at + TOK
                else:
                    window_loads.append((source.at[pl.ds(first, SHORT)], win.at[pl.ds(at, SHORT)]))
                    first, at = first + SHORT, at + SHORT
    window_loads = copies_of(window_loads, win_sem)
    names = ("wk", "wv", "wq", "wo", "ogs", "ogl", "wg", "wu", "wd")
    loads = dict(zip(names, copies_of((
        (wk_h, wk), (wv_h, wv), (wq_h, wq), (wo_h, wo),
        (og_h.at[pl.ds(short_at, SHORT)], og.at[pl.ds(0, SHORT)]),
        (og_h.at[pl.ds(long_at, LONG)], og.at[pl.ds(SHORT, LONG)]),
        (wg_h, wg), (wu_h, wu), (wd_h, wd),
    ), sems)))
    stores = Stores(out_sem)
    bias_s[...] = mask_bias("short", chip, core)
    bias_l[...] = mask_bias("long", chip, core)
    gain_a = ga[...].reshape(1, D)
    gain_m = gm[...].reshape(1, D)
    for copy in window_loads:
        copy.wait()

    def normalise(step, carry):
        rows = pl.ds(pl.multiple_of(step * NORM_ROWS, 16), NORM_ROWS)
        x = win[rows, :].astype(f32)
        scale = lax.rsqrt(jnp.mean(x * x, axis=-1, keepdims=True) + epsilon)
        norm[rows, :] = (x * scale * gain_a).astype(bf16)
        return carry

    lax.fori_loop(0, 2 * SIDE // NORM_ROWS, normalise, 0)
    stores.start(norm, norm_h)
    loads["wk"].wait()
    loads["wv"].wait()
    for side in range(2):
        normed = norm[side * SIDE : (side + 1) * SIDE, :]
        kv[:, :HD] = mm(normed, wk[...])
        kv[:, HD:] = mm(normed, wv[...])
        for number, group in enumerate(window_groups()):
            rows = slice(number * SHORT, (number + 1) * SHORT)
            cos, sin = group_tables(tables, chip, core, side, group)
            low_half, high_half = kv[rows, :HALF], kv[rows, HALF:HD]
            at = key_row(side, group)
            k[at : at + SHORT, :HALF] = (low_half * cos - high_half * sin).astype(bf16)
            k[at : at + SHORT, HALF:] = (high_half * cos + low_half * sin).astype(bf16)
            v[at : at + SHORT, :] = kv[rows, HD:].astype(bf16)
            if side == 0 and number < 3:
                skv[rows, :HD] = k[at : at + SHORT, :]
                skv[rows, HD:] = v[at : at + SHORT, :]
    stores.start(k, k_h)
    stores.start(v, v_h)
    stores.start(skv.at[pl.ds(0, SHORT)], skv_h.at[pl.ds(short_at, SHORT)])
    stores.start(skv.at[pl.ds(SHORT, LONG)], skv_h.at[pl.ds(long_at, LONG)])

    loads["wq"].wait()
    query_raw = mm(norm[:TOK, :], wq[...])
    for number in range(3):
        rows = slice(number * SHORT, (number + 1) * SHORT)
        cos, sin = group_tables(tables, chip, core, 0, window_groups()[number])
        for head in range(HEADS):
            low_half = query_raw[rows, head * HD : head * HD + HALF]
            high_half = query_raw[rows, head * HD + HALF : (head + 1) * HD]
            at = head * SHORT if number == 0 else HEADS * SHORT + head * LONG + (number - 1) * SHORT
            q[at : at + SHORT, :HALF] = (low_half * cos - high_half * sin).astype(bf16) * bf16(HD**-0.5)
            q[at : at + SHORT, HALF:] = (high_half * cos + low_half * sin).astype(bf16) * bf16(HD**-0.5)
    stores.start(q, q_h)

    for kind, rows, key_at, width, query_at, row_at in KINDS:
        bias = bias_s if kind == "short" else bias_l
        count = HEADS * rows
        scores_all[:count, :width] = mm_nt(q[query_at : query_at + count, :], k[key_at : key_at + width, :])
        for head in range(HEADS):
            here = slice(head * rows, (head + 1) * rows)
            scores = scores_all[here, :width] + bias[...]
            exponent = jnp.exp(scores - jnp.max(scores, axis=-1, keepdims=True))
            share = 1.0 / jnp.sum(exponent, axis=-1, keepdims=True)
            probs_all[here, :width] = (exponent * share).astype(bf16)
        mixed_all = mm(probs_all[:count, :width], v[key_at : key_at + width, :]).astype(bf16)
        for head in range(HEADS):
            mixed[row_at : row_at + rows, head * HD : (head + 1) * HD] = mixed_all[
                head * rows : (head + 1) * rows, :
            ]

    loads["wo"].wait()
    resid = win[:TOK, :].astype(f32) + mm(mixed[...], wo[...])
    scale = lax.rsqrt(jnp.mean(resid * resid, axis=-1, keepdims=True) + epsilon)
    unit = resid * scale
    normed_mlp = (unit * gain_m).astype(bf16)
    for name in ("ogs", "ogl", "wg", "wu", "wd"):
        loads[name].wait()
    grad_out = og[...]
    for half in range(2):
        acts[half, :, AT_MIXED:AT_NORMED] = mixed[:, half * 2 * HD : (half + 1) * 2 * HD]
        acts[half, :, AT_NORMED:AT_OUT] = normed_mlp
        acts[half, :, AT_OUT:AT_BRANCH] = grad_out
    out_sum[...] = resid
    grad_sum[...] = jnp.zeros((TOK, D), f32)

    def feed_forward(chunk, carry):
        cols = pl.ds(pl.multiple_of(chunk * FF_CHUNK, FF_CHUNK), FF_CHUNK)
        gate = mm(normed_mlp, wg[:, cols])
        up = mm(normed_mlp, wu[:, cols])
        sig = jax.nn.sigmoid(gate)
        silu = gate * sig
        act = (silu * up).astype(bf16)
        grad_act = mm_nt(grad_out, wd[cols, :])
        grad_gate = (grad_act * up * sig * (1.0 + gate * (1.0 - sig))).astype(bf16)
        grad_up = (grad_act * silu).astype(bf16)
        out_sum[...] += mm(act, wd[cols, :])
        grad_sum[...] += mm_nt(grad_gate, wg[:, cols]) + mm_nt(grad_up, wu[:, cols])
        half, at = chunk // 2, chunk % 2 * FF_CHUNK
        for first, values in ((0, act), (AT_GATE, grad_gate), (AT_UP, grad_up)):
            acts[half, :, pl.ds(pl.multiple_of(first + at, FF_CHUNK), FF_CHUNK)] = values
        return carry

    lax.fori_loop(0, FF // FF_CHUNK, feed_forward, 0, unroll=1)
    block_out, grad_normed = out_sum[...], grad_sum[...]
    stores.start(acts.at[1 - core, :, pl.ds(0, AT_BRANCH)], send_h.at[:, pl.ds(0, AT_BRANCH)])
    stores.start(acts.at[core, :, pl.ds(0, AT_BRANCH)], keep_h.at[:, pl.ds(0, AT_BRANCH)])
    ggain_o[...] = jnp.sum(grad_normed * unit, axis=0, keepdims=True)
    scaled = grad_normed * gain_m
    grad_resid = grad_out.astype(f32) + scale * (
        scaled - unit * jnp.mean(scaled * unit, axis=-1, keepdims=True)
    )
    grad_branch = grad_resid.astype(bf16)
    for half in range(2):
        acts[half, :, AT_BRANCH:] = grad_branch
    rest = pl.ds(AT_BRANCH, ACTS - AT_BRANCH)
    stores.start(acts.at[1 - core, :, rest], send_h.at[:, rest])
    stores.start(acts.at[core, :, rest], keep_h.at[:, rest])
    gres[...] = grad_resid
    stores.start(gres, gres_h)
    bo[...] = block_out.astype(bf16)
    stores.start(bo.at[pl.ds(0, SHORT)], bo_h.at[pl.ds(short_at, SHORT)])
    stores.start(bo.at[pl.ds(SHORT, LONG)], bo_h.at[pl.ds(long_at, LONG)])
    grad_mixed = mm_nt(grad_branch, wo[...]).astype(bf16)
    for head in range(HEADS):
        cols = slice(head * HD, (head + 1) * HD)
        gmix[head * SHORT : (head + 1) * SHORT, :] = grad_mixed[:SHORT, cols]
        at = HEADS * SHORT + head * LONG
        gmix[at : at + LONG, :] = grad_mixed[SHORT:, cols]
    stores.start(gmix, gmix_h)
    stores.wait()


def backward_kernel(
    tables, ga, q_h, k_h, v_h, gmix_h, norm_h, wq_h, wk_h, wv_h,
    mine_h, other_h, gnq_h, keep_h, send_h,
    q, k, v, gmix, norm, wq, wk, wv, scores_all, gp_all, probs_all, gs_all, ret, gq, gnq, b, bias_s, bias_l,
    sems, out_sem,
):
    chip, core = place()
    loads = copies_of((
        (q_h, q), (k_h, k), (gmix_h, gmix), (v_h, v), (norm_h, norm), (wq_h, wq), (wk_h, wk), (wv_h, wv),
    ), sems)
    stores = Stores(out_sem)
    bias_s[...] = mask_bias("short", chip, core)
    bias_l[...] = mask_bias("long", chip, core)
    for copy in loads[:4]:
        copy.wait()
    for kind, rows, key_at, width, query_at, row_at in KINDS:
        bias = bias_s if kind == "short" else bias_l
        keys = k[key_at : key_at + width, :]
        count = HEADS * rows
        stack = slice(query_at, query_at + count)
        scores_all[:count, :width] = mm_nt(q[stack, :], keys)
        gp_all[:count, :width] = mm_nt(gmix[stack, :], v[key_at : key_at + width, :])
        for head in range(HEADS):
            here = slice(head * rows, (head + 1) * rows)
            scores = scores_all[here, :width] + bias[...]
            exponent = jnp.exp(scores - jnp.max(scores, axis=-1, keepdims=True))
            probs = exponent * (1.0 / jnp.sum(exponent, axis=-1, keepdims=True))
            probs_all[here, :width] = probs.astype(bf16)
            grad_probs = gp_all[here, :width]
            inner = jnp.sum(probs * grad_probs, axis=-1, keepdims=True)
            gs_all[here, :width] = (probs * (grad_probs - inner)).astype(bf16)
        grad_queries = mm(gs_all[:count, :width], keys) * (HD**-0.5)
        for head in range(HEADS):
            for part in range(rows // SHORT):
                number = 0 if kind == "short" else 1 + part
                cos, sin = group_tables(tables, chip, core, 0, window_groups()[number])
                at = head * rows + part * SHORT
                low_half = grad_queries[at : at + SHORT, :HALF]
                high_half = grad_queries[at : at + SHORT, HALF:]
                to = slice(row_at + part * SHORT, row_at + (part + 1) * SHORT)
                gq[to, head * HD : head * HD + HALF] = (low_half * cos + high_half * sin).astype(bf16)
                gq[to, head * HD + HALF : (head + 1) * HD] = (high_half * cos - low_half * sin).astype(bf16)
        grad_keys = mm_tn(gs_all[:count, :width], q[stack, :])
        grad_values = mm_tn(probs_all[:count, :width], gmix[stack, :])
        for side in range(2):
            for number, group in enumerate(window_groups()):
                if group[1] != kind:
                    continue
                at = key_row(side, group) - key_at
                cos, sin = group_tables(tables, chip, core, side, group)
                low_half = grad_keys[at : at + SHORT, :HALF]
                high_half = grad_keys[at : at + SHORT, HALF:]
                to = slice(number * SHORT, (number + 1) * SHORT)
                ret[side, to, :HALF] = (low_half * cos + high_half * sin).astype(bf16)
                ret[side, to, HALF:HD] = (high_half * cos - low_half * sin).astype(bf16)
                ret[side, to, HD:] = grad_values[at : at + SHORT, :].astype(bf16)
    stores.start(ret.at[0], mine_h)
    stores.start(ret.at[1], other_h)
    for copy in loads[4:]:
        copy.wait()
    gnq[...] = mm_nt(gq[...], wq[...])
    stores.start(gnq, gnq_h)
    grad_gain = jnp.sum(gnq[...] * norm[:TOK, :].astype(f32), axis=0, keepdims=True)

    def gain_part(step, total):
        side, first = step // 4, pl.multiple_of(step % 4 * (SIDE // 4), 16)
        rows = pl.ds(first, SIDE // 4)
        grad_normed = mm_nt(ret[side, rows, :HD], wk[...]) + mm_nt(ret[side, rows, HD:], wv[...])
        here = norm[pl.ds(pl.multiple_of(side * SIDE + first, 16), SIDE // 4), :].astype(f32)
        return total + jnp.sum(grad_normed * here, axis=0, keepdims=True)

    grad_gain = lax.fori_loop(0, 8, gain_part, grad_gain, unroll=2)
    grad_gain = grad_gain / ga[...].reshape(1, D)

    def put(half, at, block):
        for part in range(block.shape[1] // HALF):
            row = at + part * D
            b[half, row : row + D, :] = block[:, part * HALF : (part + 1) * HALF].astype(bf16)

    b[0, B_GAIN:, :] = jnp.zeros((B_ROWS - B_GAIN, HALF), bf16)
    b[1, B_GAIN:, :] = jnp.zeros((B_ROWS - B_GAIN, HALF), bf16)
    for part in range(D // HALF):
        b[0, B_GAIN + 16 * part : B_GAIN + 16 * part + 16, :] = jnp.broadcast_to(
            grad_gain[:, part * HALF : (part + 1) * HALF], (16, HALF)
        ).astype(bf16)
    for half in range(2):
        put(half, B_QUERY, mm_tn(norm[:TOK, :], gq[:, half * 2 * HD : (half + 1) * 2 * HD]))
    both = mm_tn(norm[:SIDE, :], ret[0]) + mm_tn(norm[SIDE:, :], ret[1])
    for half in range(2):
        put(half, B_KV, both[:, half * HD : (half + 1) * HD])
    stores.start(b.at[1 - core], send_h)
    stores.start(b.at[core], keep_h)
    stores.wait()


def pieces_out(stores, pieces, outs):
    me = lax.axis_index("dp")
    for step, out in enumerate(outs):
        stores.start(pieces.at[lax.rem(me + step, DP)], out)


def halves_kernel(ggain, keep_h, recv_h, p0_h, p1_h, p2_h, p3_h, xz_h, x, pieces, xz, sems, out_sem):
    copies = copies_of(((keep_h, x.at[pl.ds(0, TOK)]), (recv_h, x.at[pl.ds(TOK, TOK)])), sems)
    stores = Stores(out_sem)
    for copy in copies:
        copy.wait()

    def write(at, values):
        done, rows = 0, values.shape[0]
        while done < rows:
            row = at + done
            if row < A_DP:
                piece, inner = row // A_DP_PIECE, row % A_DP_PIECE
                size = min(rows - done, A_DP_PIECE - inner)
                pieces[piece, inner : inner + size, :] = values[done : done + size, :]
            else:
                piece, inner = (row - A_DP) // A_XZ_PIECE, (row - A_DP) % A_XZ_PIECE
                size = min(rows - done, A_XZ_PIECE - inner)
                xz[piece, inner : inner + size, :] = values[done : done + size, :]
            done += size

    def put(at, block):
        rows = block.shape[0]
        for part in range(block.shape[1] // HALF):
            write(at + part * rows, block[:, part * HALF : (part + 1) * HALF].astype(bf16))

    normed = x[:, AT_NORMED:AT_OUT]
    for chunk in range(2):
        cols = slice(AT_GATE + chunk * FF_CHUNK, AT_GATE + (chunk + 1) * FF_CHUNK)
        put(A_GATE + chunk * 4 * D, mm_tn(normed, x[:, cols]))
    for chunk in range(2):
        cols = slice(AT_UP + chunk * FF_CHUNK, AT_UP + (chunk + 1) * FF_CHUNK)
        put(A_UP + chunk * 4 * D, mm_tn(normed, x[:, cols]))
        if chunk == 0:
            pieces_out(stores, pieces, (p0_h, p1_h, p2_h, p3_h))
    put(A_DOWN, mm_tn(x[:, :AT_GATE], x[:, AT_OUT:AT_BRANCH]))
    put(A_PROJ, mm_tn(x[:, AT_MIXED:AT_NORMED], x[:, AT_BRANCH:]))
    for part in range(D // HALF):
        write(A_GAIN + 16 * part, jnp.broadcast_to(
            ggain[:, part * HALF : (part + 1) * HALF], (16, HALF)
        ).astype(bf16))
    end = A_GAIN + 16 * (D // HALF)
    write(end, jnp.zeros((A_ROWS - end, HALF), bf16))
    stores.start(xz, xz_h)
    stores.wait()


def chip_sum_kernel(keep, recv, p0_h, p1_h, p2_h, p3_h, pieces, out_sem):
    stores = Stores(out_sem)
    for piece in range(DP):
        rows = slice(piece * B_PIECE, (piece + 1) * B_PIECE)
        pieces[piece] = (keep[rows, :].astype(f32) + recv[rows, :].astype(f32)).astype(bf16)
    pieces_out(stores, pieces, (p0_h, p1_h, p2_h, p3_h))
    stores.wait()


def first_sum_kernel(
    a0, a1, a2, a3, b0, b1, b2, b3, xz, out_xz, p0_h, p1_h, p2_h, p3_h, pieces, out_sem
):
    stores = Stores(out_sem)
    for piece in range(DP):
        rows = slice(piece * A_XZ_BLOCK, (piece + 1) * A_XZ_BLOCK)
        total = xz[0, rows, :].astype(f32)
        for chip in range(1, CHIPS):
            total = total + xz[chip, rows, :].astype(f32)
        pieces[piece] = total.astype(bf16)
    pieces_out(stores, pieces, (p0_h, p1_h, p2_h, p3_h))
    for chip in range(CHIPS):
        for at, size, parts in ((0, A_DP_BLOCK, (a0, a1, a2, a3)), (A_DP_BLOCK, B_BLOCK, (b0, b1, b2, b3))):
            rows = slice(chip * size, (chip + 1) * size)
            total = (parts[0][rows, :].astype(f32) + parts[1][rows, :].astype(f32)) + (
                parts[2][rows, :].astype(f32) + parts[3][rows, :].astype(f32)
            )
            out_xz[chip, at : at + size, :] = total.astype(bf16)
    stores.wait()


def second_sum_kernel(xz, c0, c1, c2, c3, copies_h, own, total, out_sem):
    stores = Stores(out_sem)
    rest = (
        (c0[...].astype(f32) + c1[...].astype(f32)) + (c2[...].astype(f32) + c3[...].astype(f32))
    ).astype(bf16)
    own[...] = rest[JOINED:, :]
    value = xz[0].astype(f32)
    for chip in range(1, CHIPS):
        value = value + xz[chip].astype(f32)
    total[: XZ_FIRST - JOINED, :] = value.astype(bf16)
    total[XZ_FIRST - JOINED :, :] = rest[:JOINED, :]
    for chip in range(CHIPS):
        stores.start(total, copies_h.at[chip])
    stores.wait()


def spread_kernel(d0, d1, d2, d3, copies_h, rows, out_sem):
    stores = Stores(out_sem)
    me = lax.axis_index("dp")
    for step, part in enumerate((d0, d1, d2, d3)):
        rows[lax.rem(me + DP - step, DP)] = part[...]
    for chip in range(CHIPS):
        stores.start(rows, copies_h.at[chip])
    stores.wait()


def window_sum_kernel(mine, other, known, r1, r2, r3):
    at = 0
    for out in (known, r1, r2, r3):
        rows = slice(at, at + out.shape[0])
        out[...] = (mine[rows, :].astype(f32) + other[rows, :].astype(f32)).astype(bf16)
        at += out.shape[0]


def turn_back_kernel(known, c1, c2, c3, own, back, far_back):
    ahead = lax.axis_index("z")
    own_sum = known[:TOK, :].astype(f32)
    back_sum = known[TOK : 2 * TOK, :].astype(f32)
    far_sum = known[2 * TOK :, :].astype(f32)
    for step, came in enumerate((c1, c2, c3), 1):
        same = (ahead + step < 4).astype(f32)
        near, far = came[:TOK, :].astype(f32), came[TOK:, :].astype(f32)
        own_sum = own_sum + near * same
        back_sum = back_sum + near * (1.0 - same)
        back_sum = jnp.concatenate([back_sum[:SHORT, :] + far * same, back_sum[SHORT:, :]], axis=0)
        far_sum = far_sum + far * (1.0 - same)
    own[...] = own_sum
    back[...] = back_sum.astype(bf16)
    far_back[...] = far_sum.astype(bf16)


def token_grad_kernel(lengths, ga, own, back, far_back, gnq, gres, tokens_h, wk, wv, out_h, x, out, sems):
    short_at, long_at = starts(lengths)
    loads = copies_of((
        (tokens_h.at[pl.ds(short_at, SHORT)], x.at[pl.ds(0, SHORT)]),
        (tokens_h.at[pl.ds(long_at, LONG)], x.at[pl.ds(SHORT, LONG)]),
    ), sems)
    total = own[...] + back[...].astype(f32)
    total = jnp.concatenate([total[:SHORT, :] + far_back[...].astype(f32), total[SHORT:, :]], axis=0).astype(bf16)
    grad_normed = gnq[...] + mm_nt(total[:, :HD], wk[...]) + mm_nt(total[:, HD:], wv[...])
    for copy in loads:
        copy.wait()
    wide = x[...].astype(f32)
    scale = lax.rsqrt(jnp.mean(wide * wide, axis=-1, keepdims=True) + epsilon)
    unit = wide * scale
    scaled = grad_normed * ga[...].reshape(1, D)
    out[...] = gres[...] + scale * (scaled - unit * jnp.mean(scaled * unit, axis=-1, keepdims=True))
    stores = copies_of((
        (out.at[pl.ds(0, SHORT)], out_h.at[pl.ds(short_at, SHORT)]),
        (out.at[pl.ds(SHORT, LONG)], out_h.at[pl.ds(long_at, LONG)]),
    ), sems, 2)
    for copy in stores:
        copy.wait()


def unpack_kernel(
    e0_h, e1_h, e2_h, e3_h, f_h, o0_h, o1_h, o2_h, o3_h, p_h,
    gain_a_o, gain_m_o, gate_h, up_h, down_h, proj_h, query_h, key_h, value_h,
    a_dp, a_xz, b, gate, up, down, proj, query, key, value, sems, out_sem,
):
    mine, me = lax.axis_index("core"), lax.axis_index("dp")
    sides = ((mine, (e0_h, e1_h, e2_h, e3_h), f_h), (1 - mine, (o0_h, o1_h, o2_h, o3_h), p_h))
    firsts, seconds, thirds = [], [], []
    for side, parts, xz_h in sides:
        for step, part in enumerate(parts):
            dp = lax.rem(me + DP - step, DP)
            firsts.append((part.at[:, pl.ds(0, A_DP_BLOCK)], a_dp.at[side, dp]))
            seconds.append((part.at[:, pl.ds(A_DP_BLOCK, B_BLOCK)], b.at[side, dp]))
            thirds.append((part.at[:, pl.ds(XZ_FIRST - JOINED, JOINED)], a_xz.at[side, :, dp, pl.ds(0, JOINED)]))
        thirds.append((xz_h, a_xz.at[side, :, :, pl.ds(JOINED, DP_FIRST)]))
    loads = copies_of(firsts + seconds + thirds, sems)
    stores = Stores(out_sem)

    def pieces_of(core, at, rows, in_b):
        done = 0
        while done < rows:
            row = at + done
            if in_b:
                source, size = b, B_BLOCK
                index = (core, row // B_PIECE, row % B_PIECE // B_BLOCK)
            elif row < A_DP:
                source, size = a_dp, A_DP_BLOCK
                index = (core, row // A_DP_PIECE, row % A_DP_PIECE // A_DP_BLOCK)
            else:
                row = row - A_DP
                source, size = a_xz, A_XZ_BLOCK
                index = (core, row // A_XZ_PIECE, row % A_XZ_PIECE // A_XZ_BLOCK)
            inner = row % size
            size = min(rows - done, size - inner)
            yield done, size, source[index + (slice(inner, inner + size), slice(None))].astype(f32)
            done += size

    def unpack(target, at, rows, in_b, place_of, count, cores=(0, 1)):
        for core in cores:
            for part in range(count):
                row, col = place_of(core, part)
                for done, size, values in pieces_of(core, at + part * rows, rows, in_b):
                    target[row + done : row + done + size, col : col + HALF] = values

    for copy in loads[: 2 * DP]:
        copy.wait()
    unpack(gate, A_GATE, D, False, lambda core, part: (0, core * HALF_FF + part * HALF), HALF_FF // HALF)
    stores.start(gate, gate_h)
    for copy in loads[2 * DP : 4 * DP]:
        copy.wait()
    unpack(query, B_QUERY, D, True, lambda core, part: (0, core * 2 * HD + part * HALF), 4)
    stores.start(query, query_h)
    unpack(key, B_KV, D, True, lambda core, part: (0, part * HALF), 2, (0,))
    stores.start(key, key_h)
    unpack(value, B_KV, D, True, lambda core, part: (0, part * HALF), 2, (1,))
    stores.start(value, value_h)
    for copy in loads[4 * DP :]:
        copy.wait()
    unpack(up, A_UP, D, False, lambda core, part: (0, core * HALF_FF + part * HALF), HALF_FF // HALF)
    stores.start(up, up_h)
    unpack(down, A_DOWN, HALF_FF, False, lambda core, part: (core * HALF_FF, part * HALF), D // HALF)
    stores.start(down, down_h)
    unpack(proj, A_PROJ, 2 * HD, False, lambda core, part: (core * 2 * HD, part * HALF), D // HALF)
    stores.start(proj, proj_h)
    for out, at, in_b in ((gain_a_o, B_GAIN, True), (gain_m_o, A_GAIN, False)):
        for part in range(D // HALF):
            (_, _, first), = pieces_of(0, at + 16 * part, 1, in_b)
            (_, _, second), = pieces_of(1, at + 16 * part, 1, in_b)
            out[part * HALF : (part + 1) * HALF] = (first + second).reshape(HALF)
    stores.wait()


VMEM = pl.BlockSpec(memory_space=pltpu.VMEM)
SMEM = pl.BlockSpec(memory_space=pltpu.SMEM)
ANY = pl.BlockSpec(memory_space=pl.ANY)


def shape(dims, kind=bf16):
    return jax.ShapeDtypeStruct(dims, kind)


def limit(mib):
    return pltpu.CompilerParams(vmem_limit_bytes=mib * 2**20)


def cost(flops, moved):
    return pl.CostEstimate(flops=flops, bytes_accessed=moved, transcendentals=0)


def scratch(*dims, kind=bf16):
    return pltpu.VMEM(dims, kind)


def semaphores(count):
    return pltpu.SemaphoreType.DMA((count,))


def run_forward(*operands):
    return pl.pallas_call(
        forward_kernel,
        in_specs=[SMEM] + [VMEM] * 3 + [ANY] * 16,
        out_specs=[VMEM] + [ANY] * 10,
        out_shape=[
            shape((1, D), f32),
            shape((HEADS * TOK, HD)), shape((KEYS, HD)), shape((KEYS, HD)), shape((HEADS * TOK, HD)),
            shape((2 * SIDE, D)), shape((TOK, D), f32),
            shape((TOK, D)), shape((TOK, 2 * HD)), shape((TOK, ACTS)), shape((TOK, ACTS)),
        ],
        scratch_shapes=[
            scratch(2 * SIDE, D), scratch(TOK, D), scratch(D, HEADS * HD), scratch(D, HD), scratch(D, HD),
            scratch(HEADS * HD, D), scratch(D, FF), scratch(D, FF), scratch(FF, D),
            scratch(2 * SIDE, D), scratch(HEADS * TOK, HD), scratch(KEYS, HD), scratch(KEYS, HD),
            scratch(SIDE, 2 * HD, kind=f32), scratch(HEADS * LONG, KEYS_LONG, kind=f32),
            scratch(HEADS * LONG, KEYS_LONG), scratch(TOK, HEADS * HD), scratch(HEADS * TOK, HD),
            scratch(TOK, D, kind=f32), scratch(TOK, D), scratch(TOK, 2 * HD), scratch(2, TOK, ACTS),
            scratch(SHORT, KEYS_SHORT, kind=f32), scratch(LONG, KEYS_LONG, kind=f32),
            scratch(TOK, D, kind=f32), scratch(TOK, D, kind=f32),
            semaphores(28), semaphores(9), semaphores(14),
        ],
        compiler_params=limit(58),
        cost_estimate=cost(8 * 10**9, 3 * 10**7),
        name="forward",
    )(*operands)


def run_backward(*operands):
    return pl.pallas_call(
        backward_kernel,
        in_specs=[VMEM] * 2 + [ANY] * 8,
        out_specs=[ANY] * 5,
        out_shape=[
            shape((SIDE, 2 * HD)), shape((SIDE, 2 * HD)), shape((TOK, D), f32),
            shape((B_ROWS, HALF)), shape((B_ROWS, HALF)),
        ],
        scratch_shapes=[
            scratch(HEADS * TOK, HD), scratch(KEYS, HD), scratch(KEYS, HD), scratch(HEADS * TOK, HD),
            scratch(2 * SIDE, D), scratch(D, HEADS * HD), scratch(D, HD), scratch(D, HD),
            scratch(HEADS * LONG, KEYS_LONG, kind=f32), scratch(HEADS * LONG, KEYS_LONG, kind=f32),
            scratch(HEADS * LONG, KEYS_LONG), scratch(HEADS * LONG, KEYS_LONG),
            scratch(2, SIDE, 2 * HD), scratch(TOK, HEADS * HD), scratch(TOK, D, kind=f32),
            scratch(2, B_ROWS, HALF),
            scratch(SHORT, KEYS_SHORT, kind=f32), scratch(LONG, KEYS_LONG, kind=f32),
            semaphores(8), semaphores(5),
        ],
        compiler_params=limit(54),
        cost_estimate=cost(10**12, 10**9),
        name="backward",
    )(*operands)


def run_halves(*operands):
    return pl.pallas_call(
        halves_kernel,
        in_specs=[VMEM, ANY, ANY],
        out_specs=[ANY] * 5,
        out_shape=[shape((A_DP_PIECE, HALF))] * 4 + [shape((CHIPS, A_XZ_PIECE, HALF))],
        scratch_shapes=[
            scratch(2 * TOK, ACTS), scratch(DP, A_DP_PIECE, HALF), scratch(CHIPS, A_XZ_PIECE, HALF),
            semaphores(2), semaphores(5),
        ],
        compiler_params=limit(20),
        cost_estimate=cost(2 * 10**9, 10**7),
        name="halves",
    )(*operands)


def run_chip_sum(*operands):
    return pl.pallas_call(
        chip_sum_kernel,
        in_specs=[VMEM] * 2,
        out_specs=[ANY] * 4,
        out_shape=[shape((B_PIECE, HALF))] * 4,
        scratch_shapes=[scratch(DP, B_PIECE, HALF), semaphores(4)],
        compiler_params=limit(8),
        cost_estimate=cost(0, 0),
        name="chip_sum",
    )(*operands)


def run_first_sum(*operands):
    return pl.pallas_call(
        first_sum_kernel,
        in_specs=[VMEM] * 9,
        out_specs=[VMEM] + [ANY] * 4,
        out_shape=[shape((CHIPS, A_DP_BLOCK + B_BLOCK, HALF))] + [shape((A_XZ_BLOCK, HALF))] * 4,
        scratch_shapes=[scratch(DP, A_XZ_BLOCK, HALF), semaphores(4)],
        compiler_params=limit(12),
        cost_estimate=cost(10**6, 8 * 10**6),
        name="first_sum",
    )(*operands)


def run_second_sum(*operands):
    return pl.pallas_call(
        second_sum_kernel,
        in_specs=[VMEM] * 5,
        out_specs=[ANY, VMEM],
        out_shape=[shape((CHIPS, XZ_FIRST, HALF)), shape((DP_FIRST, HALF))],
        scratch_shapes=[scratch(XZ_FIRST, HALF), semaphores(CHIPS)],
        compiler_params=limit(4),
        cost_estimate=cost(10**6, 10**6),
        name="second_sum",
    )(*operands)


def run_spread(*operands):
    return pl.pallas_call(
        spread_kernel,
        in_specs=[VMEM] * 4,
        out_specs=ANY,
        out_shape=shape((CHIPS, DP, DP_FIRST, HALF)),
        scratch_shapes=[scratch(DP, DP_FIRST, HALF), semaphores(CHIPS)],
        compiler_params=limit(4),
        cost_estimate=cost(0, 10**6),
        name="spread",
    )(*operands)


def run_unpack(*operands):
    return pl.pallas_call(
        unpack_kernel,
        in_specs=[ANY] * 10,
        out_specs=[VMEM] * 2 + [ANY] * 7,
        out_shape=[
            shape((D,), f32), shape((D,), f32), shape((D, FF), f32), shape((D, FF), f32),
            shape((FF, D), f32), shape((HEADS * HD, D), f32), shape((D, HEADS * HD), f32),
            shape((D, HD), f32), shape((D, HD), f32),
        ],
        scratch_shapes=[
            scratch(2, DP, CHIPS, A_DP_BLOCK, HALF), scratch(2, CHIPS, DP, A_XZ_BLOCK, HALF),
            scratch(2, DP, CHIPS, B_BLOCK, HALF),
            scratch(D, FF, kind=f32), scratch(D, FF, kind=f32), scratch(FF, D, kind=f32),
            scratch(HEADS * HD, D, kind=f32), scratch(D, HEADS * HD, kind=f32), scratch(D, HD, kind=f32),
            scratch(D, HD, kind=f32), semaphores(26), semaphores(7),
        ],
        compiler_params=limit(40),
        cost_estimate=cost(0, 3 * 10**7),
        name="unpack",
    )(*operands)


def run_window_sum(*operands):
    return pl.pallas_call(
        window_sum_kernel,
        in_specs=[VMEM] * 2,
        out_specs=[VMEM] * 4,
        out_shape=[shape((KNOWN, 2 * HD)), *[shape((ROUND, 2 * HD))] * 3],
        compiler_params=limit(8),
        cost_estimate=cost(0, 10**6),
        name="window_sum",
    )(*operands)


def run_turn_back(*operands):
    return pl.pallas_call(
        turn_back_kernel,
        in_specs=[VMEM] * 4,
        out_specs=[VMEM] * 3,
        out_shape=[shape((TOK, 2 * HD), f32), shape((TOK, 2 * HD)), shape((SHORT, 2 * HD))],
        compiler_params=limit(8),
        cost_estimate=cost(10**12, 10**9),
        name="turn_back",
    )(*operands)


def run_token_grad(*operands):
    return pl.pallas_call(
        token_grad_kernel,
        in_specs=[SMEM] + [VMEM] * 6 + [ANY] + [VMEM] * 2,
        out_specs=ANY,
        out_shape=shape((TOK, D), f32),
        scratch_shapes=[scratch(TOK, D), scratch(TOK, D, kind=f32), semaphores(4)],
        compiler_params=limit(12),
        cost_estimate=cost(10**6, 10**6),
        name="token_grad",
    )(*operands)


def swap_cores(array):
    return lax.ppermute(array, "core", [(0, 1), (1, 0)])


def gather_dp(pieces):
    got = [pieces[0]]
    for step in range(1, DP):
        got.append(lax.ppermute(pieces[step], "dp", [(i, (i + step) % DP) for i in range(DP)]))
    return got


def shards(
    tokens, lengths, w_query, w_key, w_value, w_output, w_gate, w_up, w_down, gain_attn, gain_mlp, out_grad
):
    short_first = lengths[0, 0] == SHORT_LEN

    slots = tokens[0]
    short_at = jnp.where(short_first, 0, LONG)

    def short_of(rows):
        return lax.dynamic_slice_in_dim(rows, short_at, SHORT, 0)

    own_short = short_of(slots)
    back = lax.ppermute(slots, "x", [(i, i + 1) for i in range(3)])
    back_short = lax.ppermute(own_short, "x", [(i, i + 2) for i in range(2)])
    here = jnp.concatenate([slots, short_of(back)], axis=0)
    there = jnp.concatenate([back, back_short], axis=0)
    ahead = lax.axis_index("z")
    rounds = [
        lax.ppermute(
            jnp.where(ahead + step < 4, here, there), "z", [(i, (i + step) % 4) for i in range(4)]
        )
        for step in range(1, 4)
    ]
    known = jnp.concatenate([slots, there], axis=0)
    window = [known, *rounds, *[swap_cores(part) for part in (known, *rounds)]]
    tables = jnp.asarray(rotary_tables())
    (
        grad_gain_mlp, q, k, v, gmix, norm, grad_resid, block_out, shared_kv, kept, sent,
    ) = run_forward(
        lengths, tables, gain_attn, gain_mlp, *window, out_grad[0],
        w_query, w_key, w_value, w_output, w_gate, w_up, w_down,
    )
    *a_pieces, a_xz = run_halves(grad_gain_mlp, kept, swap_cores(sent))
    q, a_xz = lax.optimization_barrier((q, a_xz))
    a_xz = lax.all_to_all(a_xz, CHIP, 0, 0, tiled=True)
    a_got = gather_dp(a_pieces)
    mine, other, grad_normed_q, b_kept, b_sent = run_backward(
        tables, gain_attn, q, k, v, gmix, norm, w_query, w_key, w_value
    )
    b_kept, b_sent, *a_got = lax.optimization_barrier((b_kept, b_sent, *a_got))
    b_pieces = run_chip_sum(b_kept, swap_cores(b_sent))
    b_got = gather_dp(b_pieces)

    other = swap_cores(other)
    b_got[1], other = lax.optimization_barrier((b_got[1], other))
    known_back, *round_back = run_window_sum(mine, other)
    came = [
        lax.ppermute(rows, "z", [(i, (i - step) % 4) for i in range(4)]) for step, rows in enumerate(round_back, 1)
    ]
    first, *c_pieces = run_first_sum(*a_got, *b_got, a_xz)
    c_got = gather_dp(c_pieces)
    first = lax.all_to_all(first, CHIP, 0, 0, tiled=True)
    own_back, for_back, for_far_back = run_turn_back(known_back, *came)
    copies, own_xz = run_second_sum(first, *c_got)
    copies, for_back, for_far_back = lax.optimization_barrier((copies, for_back, for_far_back))
    dp_part = lax.all_to_all(copies, CHIP, 0, 0, tiled=True)
    xz_copies = run_spread(*gather_dp([own_xz] * DP))
    dp_part, xz_copies = lax.optimization_barrier((dp_part, xz_copies))
    dp_parts = gather_dp([dp_part] * DP)
    xz_parts = lax.all_to_all(xz_copies, CHIP, 0, 0, tiled=True)
    parts = [*dp_parts, xz_parts]
    from_back = lax.ppermute(for_back, "x", [(i + 1, i) for i in range(3)])
    from_far_back = lax.ppermute(for_far_back, "x", [(i + 2, i) for i in range(2)])
    *parts, from_back, from_far_back = lax.optimization_barrier((*parts, from_back, from_far_back))
    (
        total_gain_attn, total_gain_mlp, grad_gate, grad_up, grad_down, grad_proj, grad_query, grad_key, grad_value,
    ) = run_unpack(*parts, *[swap_cores(part) for part in parts])

    input_grad = run_token_grad(
        lengths, gain_attn, own_back, from_back, from_far_back, grad_normed_q, grad_resid, slots, w_key, w_value
    )
    return (
        block_out[None], shared_kv[None], input_grad[None],
        grad_query, grad_key, grad_value, grad_proj, grad_gate, grad_up, grad_down,
        total_gain_attn, total_gain_mlp,
    )


def solution(mesh):
    fine = Mesh(mesh.devices.reshape(4, 4, 2, 4), ALL)
    rows = P("dp", SEQ, None)
    return jax.shard_map(
        shards,
        mesh=fine,
        in_specs=(rows, P("dp", None)) + (P(),) * 9 + (rows,),
        out_specs=(rows, rows, rows) + (P(),) * 9,
        check_vma=False,
    )
```

profile of v0, /device:TPU:3, one launch (start us, length us, event | category | flops | bytes accessed | tf_op | source)
XLA Modules:
  0.0 231.1 jit_solution(9511966263471808478)
XLA Ops:
  0.7 3.3 %collective-permute-start = (bf16[192,640]{1,0:T(8,128)(2,1)}, bf16[192,640]{1,0:T(8,128)(2,1)S(1)}, u32[]{:S(2)}, u32[]{:S(2)}) collective-permute-start(bf16[192,640]{1,0:T(8,128)(2,1)} %bitcast.9), channel_id=1, source_target_pairs={{0,32},{32,64},{64,96},{1,33},{33,65},{65,97},{2,34},{34,66},{66,9... | collective-permute-start | bytes 737288 | tf_op jit(solution)/shard_map/ppermute | solution.py:873
  4.6 0.9 dynamic-slice_bitcast_fusion
  5.5 1.9 collective-permute-start.1
  7.4 2.3 %collective-permute-done = bf16[192,640]{1,0:T(8,128)(2,1)S(1)} collective-permute-done((bf16[192,640]{1,0:T(8,128)(2,1)}, bf16[192,640]{1,0:T(8,128)(2,1)S(1)}, u32[]{:S(2)}, u32[]{:S(2)}) %collective-permute-start) | collective-permute-done | bytes 245792 | tf_op jit(solution)/shard_map/ppermute | solution.py:873
  9.8 1.1 broadcast_select_fusion
  10.9 3.8 %collective-permute-start.4 = (bf16[256,640]{1,0:T(8,128)(2,1)S(1)}, bf16[256,640]{1,0:T(8,128)(2,1)S(1)}, u32[]{:S(2)}, u32[]{:S(2)}) collective-permute-start(bf16[256,640]{1,0:T(8,128)(2,1)S(1)} %get-tuple-element.152), channel_id=1, source_target_pairs={{0,24},{8,0},{16,8},{24,16},{1,25},{9,1},{17,9},{25,17},{2,26},{10... | collective-permute-start | bytes 983048 | tf_op jit(solution)/shard_map/ppermute | solution.py:879
  15.5 2.5 %collective-permute-start.5 = (bf16[448,640]{1,0:T(8,128)(2,1)S(1)}, bf16[448,640]{1,0:T(8,128)(2,1)S(1)}, u32[]{:S(2)}, u32[]{:S(2)}) collective-permute-start(bf16[448,640]{1,0:T(8,128)(2,1)S(1)} %pad_maximum_fusion.w0_h), channel_id=1, source_target_pairs={{0,4},{4,0},{1,5},{5,1},{2,6},{6,2},{3,7},{7,3},{8,12},{12,8},{9,1... | collective-permute-start | bytes 1720328 | tf_op jit(solution)/shard_map/ppermute | solution.py:851
  18.0 3.9 %collective-permute-done.4.w3_h = bf16[256,640]{1,0:T(8,128)(2,1)S(1)} collective-permute-done((bf16[256,640]{1,0:T(8,128)(2,1)S(1)}, bf16[256,640]{1,0:T(8,128)(2,1)S(1)}, u32[]{:S(2)}, u32[]{:S(2)}) %collective-permute-start.4) | collective-permute-done | bytes 327712 | tf_op jit(solution)/shard_map/ppermute | solution.py:879
  21.9 7.8 %collective-permute-start.8 = (bf16[256,640]{1,0:T(8,128)(2,1)S(1)}, bf16[256,640]{1,0:T(8,128)(2,1)S(1)}, u32[]{:S(2)}, u32[]{:S(2)}) collective-permute-start(bf16[256,640]{1,0:T(8,128)(2,1)S(1)} %collective-permute-done.4.w3_h), channel_id=1, source_target_pairs={{0,4},{4,0},{1,5},{5,1},{2,6},{6,2},{3,7},{7,3},{8,12},{12,8},{9,1... | collective-permute-start | bytes 983048 | tf_op jit(solution)/shard_map/ppermute | solution.py:851
  29.8 2.5 %collective-permute-done.2.w1_h = bf16[256,640]{1,0:T(8,128)(2,1)S(1)} collective-permute-done((bf16[256,640]{1,0:T(8,128)(2,1)S(1)}, bf16[256,640]{1,0:T(8,128)(2,1)S(1)}, u32[]{:S(2)}, u32[]{:S(2)}) %collective-permute-start.2) | collective-permute-done | bytes 327712 | tf_op jit(solution)/shard_map/ppermute | solution.py:879
  32.2 0.9 collective-permute-start.6
  33.1 1.2 collective-permute-done.6.w5_h
  34.4 0.7 copy-done.28
  35.1 21.7 %forward.1 = (f32[1,640]{1,0:T(1,128)}, bf16[768,256]{1,0:T(8,128)(2,1)}, bf16[2432,256]{1,0:T(8,128)(2,1)}, bf16[2432,256]{1,0:T(8,128)(2,1)}, bf16[768,256]{1,...) custom-call(s32[1,2]{1,0:T(1,128)} %lengths.3, ...), custom_call_target="tpu_custom_call" | custom-call | flops 8000000000 | bytes 30000000 | tf_op jit(solution)/shard_map/forward/pallas_call | solution.py:670
  57.4 4.0 %collective-permute-done.9.recv_h = bf16[192,5504]{1,0:T(8,128)(2,1)S(1)} collective-permute-done((bf16[192,5504]{1,0:T(8,128)(2,1)}, bf16[192,5504]{1,0:T(8,128)(2,1)S(1)}, u32[]{:S(2)}, u32[]{:S(2)}) %collective-permute-start.9) | collective-permute-done | bytes 2113568 | tf_op jit(solution)/shard_map/ppermute | solution.py:851
  61.5 1.6 copy-done.19
  63.7 5.4 %halves.1 = (bf16[1792,128]{1,0:T(8,128)(2,1)S(1)}, bf16[1792,128]{1,0:T(8,128)(2,1)}, bf16[1792,128]{1,0:T(8,128)(2,1)}, bf16[1792,128]{1,0:T(8,128)(2,1)}, bf16[16,704,128]{2,1,0:T(8,128)(2,1)}) custom-call(f32[1,640]{1,0:T(1,128)S(1)} %copy-done.20, bf16[192,5504]{1,0:T(8,128)(2,1)S(1)} %copy-done.19, bf16[192,5504]{1,0:T(8,128)(2,1)S(1)} %collective-permute-done.9.recv_h), custom_call_target="tpu_custom_call" | custom-call | flops 2000000000 | bytes 10000000 | tf_op jit(solution)/shard_map/halves/pallas_call | solution.py:723
  69.1 7.0 %all-to-all-start = ((bf16[16,704,128]{2,1,0:T(8,128)(2,1)}), bf16[16,704,128]{2,1,0:T(8,128)(2,1)}, u32[]{:S(2)}, u32[]{:S(2)}) async-start(bf16[16,704,128]{2,1,0:T(8,128)(2,1)} %get-tuple-element.119), calls=%async_computation | async-start | bytes 5767168 | tf_op jit(solution)/shard_map/all_to_all | solution.py:895
  76.2 1.3 collective-permute-start.10
  77.5 2.6 %collective-permute-start.11 = (bf16[1792,128]{1,0:T(8,128)(2,1)}, bf16[1792,128]{1,0:T(8,128)(2,1)}, u32[]{:S(2)}, u32[]{:S(2)}) collective-permute-start(bf16[1792,128]{1,0:T(8,128)(2,1)} %get-tuple-element.99), channel_id=1, source_target_pairs={{0,2},{1,3},{2,0},{3,1},{4,6},{5,7},{6,4},{7,5},{8,10},{9,11},{10,... | collective-permute-start | bytes 1376264 | tf_op jit(solution)/shard_map/ppermute | solution.py:857
  80.1 1.1 collective-permute-start.12
  81.1 14.7 %backward.1 = (bf16[1216,512]{1,0:T(8,128)(2,1)}, bf16[1216,512]{1,0:T(8,128)(2,1)}, f32[192,640]{1,0:T(8,128)}, bf16[4096,128]{1,0:T(8,128)(2,1)}, bf16[4096,128]{1,0:T(8,128)(2,1)}) custom-call(f32[4,64,128]{2,1,0:T(8,128)} %constant.28.clone.tables, f32[640]{0:T(1024)} %ga.5, bf16[768,256]{1,0:T(8,128)(2,1)} %get-tuple-element.89.q_h, ...), custom_call_target="tpu_custom_call" | custom-call | flops 999999995904 | bytes 1000000000 | tf_op jit(solution)/shard_map/backward/pallas_call | solution.py:698
  95.9 3.9 %collective-permute-done.11.a2 = bf16[1792,128]{1,0:T(8,128)(2,1)} collective-permute-done((bf16[1792,128]{1,0:T(8,128)(2,1)}, bf16[1792,128]{1,0:T(8,128)(2,1)}, u32[]{:S(2)}, u32[]{:S(2)}) %collective-permute-start.11) | collective-permute-done | bytes 458784 | tf_op jit(solution)/shard_map/ppermute | solution.py:857
  99.8 1.8 collective-permute-start.13
  101.7 2.5 %collective-permute-done.13.recv = bf16[4096,128]{1,0:T(8,128)(2,1)S(1)} collective-permute-done((bf16[4096,128]{1,0:T(8,128)(2,1)}, bf16[4096,128]{1,0:T(8,128)(2,1)S(1)}, u32[]{:S(2)}, u32[]{:S(2)}) %collective-permute-start.13) | collective-permute-done | bytes 1048608 | tf_op jit(solution)/shard_map/ppermute | solution.py:851
  104.2 1.2 copy-done.3
  105.8 1.0 collective-permute-start.14
  106.8 2.1 collective-permute-start.19
  108.9 1.3 collective-permute-start.20
  110.2 4.5 %collective-permute-done.14.b1 = bf16[1024,128]{1,0:T(8,128)(2,1)S(1)} collective-permute-done((bf16[1024,128]{1,0:T(8,128)(2,1)S(1)}, bf16[1024,128]{1,0:T(8,128)(2,1)S(1)}, u32[]{:S(2)}, u32[]{:S(2)}) %collective-permute-start.14) | collective-permute-done | bytes 262176 | tf_op jit(solution)/shard_map/ppermute | solution.py:857
  114.7 0.9 window_sum.1
  115.6 2.3 collective-permute-start.16
  119.1 1.5 collective-permute-done.19.b2
  120.6 4.2 %first_sum.1 = (bf16[16,176,128]{2,1,0:T(8,128)(2,1)}, bf16[176,128]{1,0:T(8,128)(2,1)S(1)}, bf16[176,128]{1,0:T(8,128)(2,1)}, bf16[176,128]{1,0:T(8,128)(2,1)}, bf16[176,128]{1,0:T(8,128)(2,1)}) custom-call(bf16[1792,128]{1,0:T(8,128)(2,1)S(1)} %get-tuple-element.111.a0, bf16[1792,128]{1,0:T(8,128)(2,1)} %collective-permute-done.10.a1, ...), custom_call_target="tpu_custom_call" | custom-call | flops 1000000 | bytes 8000000 | tf_op jit(solution)/shard_map/first_sum/pallas_call | solution.py:752
  124.8 6.7 %all-to-all-start.1 = ((bf16[16,176,128]{2,1,0:T(8,128)(2,1)}), bf16[16,176,128]{2,1,0:T(8,128)(2,1)}, u32[]{:S(2)}, u32[]{:S(2)}) async-start(bf16[16,176,128]{2,1,0:T(8,128)(2,1)} %get-tuple-element.120), calls=%async_computation.1 | async-start | bytes 1441792 | tf_op jit(solution)/shard_map/all_to_all | solution.py:912
  131.5 2.1 collective-permute-start.21
  133.6 2.3 %collective-permute-start.22 = (bf16[176,128]{1,0:T(8,128)(2,1)}, bf16[176,128]{1,0:T(8,128)(2,1)}, u32[]{:S(2)}, u32[]{:S(2)}) collective-permute-start(bf16[176,128]{1,0:T(8,128)(2,1)} %get-tuple-element.123), channel_id=1, source_target_pairs={{0,2},{1,3},{2,0},{3,1},{4,6},{5,7},{6,4},{7,5},{8,10},{9,11},{10,... | collective-permute-start | bytes 135176 | tf_op jit(solution)/shard_map/ppermute | solution.py:857
  136.5 0.7 copy-done.10
  137.2 1.4 collective-permute-done.22.c2
  138.6 1.3 collective-permute-done.23.c3
  139.9 1.4 all-to-all-done.1.xz
  141.3 2.2 second_sum.1
  143.6 6.2 %all-to-all-start.2 = ((bf16[16,192,128]{2,1,0:T(8,128)(2,1)}), bf16[16,192,128]{2,1,0:T(8,128)(2,1)S(1)}, u32[]{:S(2)}, u32[]{:S(2)}) async-start(bf16[16,192,128]{2,1,0:T(8,128)(2,1)} %get-tuple-element.128), calls=%async_computation.2 | async-start | bytes 1572864 | tf_op jit(solution)/shard_map/all_to_all | solution.py:916
  149.8 3.4 %collective-permute-start.26 = (bf16[160,128]{1,0:T(8,128)(2,1)S(1)}, bf16[160,128]{1,0:T(8,128)(2,1)S(1)}, u32[]{:S(2)}, u32[]{:S(2)}) collective-permute-start(bf16[160,128]{1,0:T(8,128)(2,1)S(1)} %get-tuple-element.129.d0), channel_id=1, source_target_pairs={{0,3},{1,0},{2,1},{3,2},{4,7},{5,4},{6,5},{7,6},{8,11},{9,8},{10,9... | collective-permute-start | bytes 122888 | tf_op jit(solution)/shard_map/ppermute | solution.py:857
  154.3 3.5 %collective-permute-done.25.d2 = bf16[160,128]{1,0:T(8,128)(2,1)S(1)} collective-permute-done((bf16[160,128]{1,0:T(8,128)(2,1)S(1)}, bf16[160,128]{1,0:T(8,128)(2,1)S(1)}, u32[]{:S(2)}, u32[]{:S(2)}) %collective-permute-start.25) | collective-permute-done | bytes 40992 | tf_op jit(solution)/shard_map/ppermute | solution.py:857
  158.3 1.6 spread.1
  160.1 6.6 %all-to-all-start.3 = ((bf16[16,4,160,128]{3,2,1,0:T(8,128)(2,1)}), bf16[16,4,160,128]{3,2,1,0:T(8,128)(2,1)S(1)}, u32[]{:S(2)}, u32[]{:S(2)}) async-start(bf16[16,4,160,128]{3,2,1,0:T(8,128)(2,1)} %spread.1), calls=%async_computation.3 | async-start | bytes 5242880 | tf_op jit(solution)/shard_map/all_to_all | solution.py:920
  166.7 3.0 %collective-permute-start.29 = (bf16[16,192,128]{2,1,0:T(8,128)(2,1)S(1)}, bf16[16,192,128]{2,1,0:T(8,128)(2,1)S(1)}, u32[]{:S(2)}, u32[]{:S(2)}) collective-permute-start(bf16[16,192,128]{2,1,0:T(8,128)(2,1)S(1)} %all-to-all-done.2.e0_h), channel_id=1, source_target_pairs={{0,3},{1,0},{2,1},{3,2},{4,7},{5,4},{6,5},{7,6},{8,11},{9,8},{10,9... | collective-permute-start | bytes 2359304 | tf_op jit(solution)/shard_map/ppermute | solution.py:857
  170.4 2.1 collective-permute-start.30
  172.5 1.3 collective-permute-start.31
  173.8 29.4 %collective-permute-done.31.far_back = bf16[64,512]{1,0:T(8,128)(2,1)S(1)} collective-permute-done((bf16[64,512]{1,0:T(8,128)(2,1)S(1)}, bf16[64,512]{1,0:T(8,128)(2,1)S(1)}, u32[]{:S(2)}, u32[]{:S(2)}) %collective-permute-start.31) | collective-permute-done | bytes 65568 | tf_op jit(solution)/shard_map/ppermute | solution.py:923
  203.9 0.9 copy-done.4
  204.8 0.9 copy-done.6
  205.7 1.9 collective-permute-done.27.e1_h
  207.6 2.8 %collective-permute-start.36 = (bf16[16,4,160,128]{3,2,1,0:T(8,128)(2,1)S(1)}, bf16[16,4,160,128]{3,2,1,0:T(8,128)(2,1)S(1)}, u32[]{:S(2)}, u32[]{:S(2)}) collective-permute-start(bf16[16,4,160,128]{3,2,1,0:T(8,128)(2,1)S(1)} %all-to-all-done.3.f_h), channel_id=1, source_target_pairs={{0,4},{4,0},{1,5},{5,1},{2,6},{6,2},{3,7},{7,3},{8,12},{12,8},{9,1... | collective-permute-start | bytes 7864328 | tf_op jit(solution)/shard_map/ppermute | solution.py:851
  211.4 0.9 copy-done.1
  212.3 1.0 copy-done.8
  213.4 1.0 copy-done.9
  214.4 1.0 copy-done.11
  215.4 1.0 copy-done.12
  216.4 1.0 copy-done.13
  217.3 0.9 copy-done.15
  218.3 2.3 token_grad.1
  220.7 10.2 %unpack.1 = (f32[640]{0:T(1024)}, f32[640]{0:T(1024)}, f32[640,2048]{1,0:T(8,128)}, f32[640,2048]{1,0:T(8,128)}, f32[2048,640]{1,0:T(8,128)}, /*index=5*/f32[102...) custom-call(bf16[16,192,128]{2,1,0:T(8,128)(2,1)S(1)} %all-to-all-done.2.e0_h, ...), custom_call_target="tpu_custom_call" | custom-call | bytes 30000000 | tf_op jit(solution)/shard_map/unpack/pallas_call | solution.py:791
  (93 shorter events, 8.4 us)
Async XLA Ops:
  0.6 14.8 %copy-start = (bf16[1,192,640]{2,1,0:T(8,128)(2,1)S(1)}, bf16[1,192,640]{2,1,0:T(8,128)(2,1)}, u32[]{:S(2)}) copy-start(bf16[1,192,640]{2,1,0:T(8,128)(2,1)} %param.13) | copy-start | bytes 737284
  0.7 9.1 %collective-permute-start = (bf16[192,640]{1,0:T(8,128)(2,1)}, bf16[192,640]{1,0:T(8,128)(2,1)S(1)}, u32[]{:S(2)}, u32[]{:S(2)}) collective-permute-start(bf16[192,640]{1,0:T(8,128)(2,1)} %bitcast.9), channel_id=1, source_target_pairs={{0,32},{32,64},{64,96},{1,33},{33,65},{65,97},{2,34},{34,66},{66,9... | collective-permute-start | bytes 737288 | tf_op jit(solution)/shard_map/ppermute | solution.py:873
  5.5 4.3 %collective-permute-start.1 = (bf16[64,640]{1,0:T(8,128)(2,1)S(1)}, bf16[64,640]{1,0:T(8,128)(2,1)S(1)}, u32[]{:S(2)}, u32[]{:S(2)}) collective-permute-start(bf16[64,640]{1,0:T(8,128)(2,1)S(1)} %dynamic-slice_bitcast_fusion), channel_id=1, source_target_pairs={{0,64},{32,96},{1,65},{33,97},{2,66},{34,98},{3,67},{35,99},{4,68}... | collective-permute-start | bytes 245768 | tf_op jit(solution)/shard_map/ppermute | solution.py:874
  10.9 11.0 %collective-permute-start.4 = (bf16[256,640]{1,0:T(8,128)(2,1)S(1)}, bf16[256,640]{1,0:T(8,128)(2,1)S(1)}, u32[]{:S(2)}, u32[]{:S(2)}) collective-permute-start(bf16[256,640]{1,0:T(8,128)(2,1)S(1)} %get-tuple-element.152), channel_id=1, source_target_pairs={{0,24},{8,0},{16,8},{24,16},{1,25},{9,1},{17,9},{25,17},{2,26},{10... | collective-permute-start | bytes 983048 | tf_op jit(solution)/shard_map/ppermute | solution.py:879
  14.7 15.0 %collective-permute-start.3 = (bf16[256,640]{1,0:T(8,128)(2,1)S(1)}, bf16[256,640]{1,0:T(8,128)(2,1)S(1)}, u32[]{:S(2)}, u32[]{:S(2)}) collective-permute-start(bf16[256,640]{1,0:T(8,128)(2,1)S(1)} %get-tuple-element.153), channel_id=1, source_target_pairs={{0,16},{8,24},{16,0},{24,8},{1,17},{9,25},{17,1},{25,9},{2,18},{10... | collective-permute-start | bytes 983048 | tf_op jit(solution)/shard_map/ppermute | solution.py:879
  14.7 17.5 %collective-permute-start.2 = (bf16[256,640]{1,0:T(8,128)(2,1)S(1)}, bf16[256,640]{1,0:T(8,128)(2,1)S(1)}, u32[]{:S(2)}, u32[]{:S(2)}) collective-permute-start(bf16[256,640]{1,0:T(8,128)(2,1)S(1)} %get-tuple-element.154), channel_id=1, source_target_pairs={{0,8},{8,16},{16,24},{24,0},{1,9},{9,17},{17,25},{25,1},{2,10},{10... | collective-permute-start | bytes 983048 | tf_op jit(solution)/shard_map/ppermute | solution.py:879
  15.5 18.9 %copy-start.21 = (bf16[448,640]{1,0:T(8,128)(2,1)}, bf16[448,640]{1,0:T(8,128)(2,1)S(1)}, u32[]{:S(2)}) copy-start(bf16[448,640]{1,0:T(8,128)(2,1)S(1)} %pad_maximum_fusion.w0_h) | copy-start | bytes 1720324
  15.5 17.6 %collective-permute-start.5 = (bf16[448,640]{1,0:T(8,128)(2,1)S(1)}, bf16[448,640]{1,0:T(8,128)(2,1)S(1)}, u32[]{:S(2)}, u32[]{:S(2)}) collective-permute-start(bf16[448,640]{1,0:T(8,128)(2,1)S(1)} %pad_maximum_fusion.w0_h), channel_id=1, source_target_pairs={{0,4},{4,0},{1,5},{5,1},{2,6},{6,2},{3,7},{7,3},{8,12},{12,8},{9,1... | collective-permute-start | bytes 1720328 | tf_op jit(solution)/shard_map/ppermute | solution.py:851
  21.9 12.4 %copy-start.23 = (bf16[256,640]{1,0:T(8,128)(2,1)}, bf16[256,640]{1,0:T(8,128)(2,1)S(1)}, u32[]{:S(2)}) copy-start(bf16[256,640]{1,0:T(8,128)(2,1)S(1)} %collective-permute-done.4.w3_h) | copy-start | bytes 983044
  21.9 11.2 %collective-permute-start.8 = (bf16[256,640]{1,0:T(8,128)(2,1)S(1)}, bf16[256,640]{1,0:T(8,128)(2,1)S(1)}, u32[]{:S(2)}, u32[]{:S(2)}) collective-permute-start(bf16[256,640]{1,0:T(8,128)(2,1)S(1)} %collective-permute-done.4.w3_h), channel_id=1, source_target_pairs={{0,4},{4,0},{1,5},{5,1},{2,6},{6,2},{3,7},{7,3},{8,12},{12,8},{9,1... | collective-permute-start | bytes 983048 | tf_op jit(solution)/shard_map/ppermute | solution.py:851
  29.7 4.7 %copy-start.24 = (bf16[256,640]{1,0:T(8,128)(2,1)}, bf16[256,640]{1,0:T(8,128)(2,1)S(1)}, u32[]{:S(2)}) copy-start(bf16[256,640]{1,0:T(8,128)(2,1)S(1)} %collective-permute-done.3.w2_h) | copy-start | bytes 983044
  29.7 3.4 %collective-permute-start.7 = (bf16[256,640]{1,0:T(8,128)(2,1)S(1)}, bf16[256,640]{1,0:T(8,128)(2,1)S(1)}, u32[]{:S(2)}, u32[]{:S(2)}) collective-permute-start(bf16[256,640]{1,0:T(8,128)(2,1)S(1)} %collective-permute-done.3.w2_h), channel_id=1, source_target_pairs={{0,4},{4,0},{1,5},{5,1},{2,6},{6,2},{3,7},{7,3},{8,12},{12,8},{9,1... | collective-permute-start | bytes 983048 | tf_op jit(solution)/shard_map/ppermute | solution.py:851
  32.2 2.1 copy-start.25
  32.2 2.1 collective-permute-start.6
  33.1 1.3 copy-start.22
  33.1 1.3 copy-start.26
  33.1 1.3 copy-start.27
  56.8 4.7 %collective-permute-start.9 = (bf16[192,5504]{1,0:T(8,128)(2,1)}, bf16[192,5504]{1,0:T(8,128)(2,1)S(1)}, u32[]{:S(2)}, u32[]{:S(2)}) collective-permute-start(bf16[192,5504]{1,0:T(8,128)(2,1)} %get-tuple-element.87), channel_id=1, source_target_pairs={{0,4},{4,0},{1,5},{5,1},{2,6},{6,2},{3,7},{7,3},{8,12},{12,8},{9,1... | collective-permute-start | bytes 6340616 | tf_op jit(solution)/shard_map/ppermute | solution.py:851
  61.5 1.6 copy-start.19
  69.1 51.5 %all-to-all-start = ((bf16[16,704,128]{2,1,0:T(8,128)(2,1)}), bf16[16,704,128]{2,1,0:T(8,128)(2,1)}, u32[]{:S(2)}, u32[]{:S(2)}) async-start(bf16[16,704,128]{2,1,0:T(8,128)(2,1)} %get-tuple-element.119), calls=%async_computation | async-start | bytes 5767168 | tf_op jit(solution)/shard_map/all_to_all | solution.py:895
  76.2 19.7 %collective-permute-start.10 = (bf16[1792,128]{1,0:T(8,128)(2,1)}, bf16[1792,128]{1,0:T(8,128)(2,1)}, u32[]{:S(2)}, u32[]{:S(2)}) collective-permute-start(bf16[1792,128]{1,0:T(8,128)(2,1)} %get-tuple-element.98), channel_id=1, source_target_pairs={{0,1},{1,2},{2,3},{3,0},{4,5},{5,6},{6,7},{7,4},{8,9},{9,10},{10,1... | collective-permute-start | bytes 1376264 | tf_op jit(solution)/shard_map/ppermute | solution.py:857
  77.5 22.4 %collective-permute-start.11 = (bf16[1792,128]{1,0:T(8,128)(2,1)}, bf16[1792,128]{1,0:T(8,128)(2,1)}, u32[]{:S(2)}, u32[]{:S(2)}) collective-permute-start(bf16[1792,128]{1,0:T(8,128)(2,1)} %get-tuple-element.99), channel_id=1, source_target_pairs={{0,2},{1,3},{2,0},{3,1},{4,6},{5,7},{6,4},{7,5},{8,10},{9,11},{10,... | collective-permute-start | bytes 1376264 | tf_op jit(solution)/shard_map/ppermute | solution.py:857
  80.1 19.8 %collective-permute-start.12 = (bf16[1792,128]{1,0:T(8,128)(2,1)}, bf16[1792,128]{1,0:T(8,128)(2,1)}, u32[]{:S(2)}, u32[]{:S(2)}) collective-permute-start(bf16[1792,128]{1,0:T(8,128)(2,1)} %get-tuple-element.100), channel_id=1, source_target_pairs={{0,3},{1,0},{2,1},{3,2},{4,7},{5,4},{6,5},{7,6},{8,11},{9,8},{10,9... | collective-permute-start | bytes 1376264 | tf_op jit(solution)/shard_map/ppermute | solution.py:857
  95.9 18.8 %copy-start.2 = (bf16[1216,512]{1,0:T(8,128)(2,1)S(1)}, bf16[1216,512]{1,0:T(8,128)(2,1)}, u32[]{:S(2)}) copy-start(bf16[1216,512]{1,0:T(8,128)(2,1)} %get-tuple-element.94.mine) | copy-start | bytes 3735556
  99.8 4.3 %collective-permute-start.13 = (bf16[4096,128]{1,0:T(8,128)(2,1)}, bf16[4096,128]{1,0:T(8,128)(2,1)S(1)}, u32[]{:S(2)}, u32[]{:S(2)}) collective-permute-start(bf16[4096,128]{1,0:T(8,128)(2,1)} %get-tuple-element.102), channel_id=1, source_target_pairs={{0,4},{4,0},{1,5},{5,1},{2,6},{6,2},{3,7},{7,3},{8,12},{12,8},{9,1... | collective-permute-start | bytes 3145736 | tf_op jit(solution)/shard_map/ppermute | solution.py:851
  101.7 8.5 %collective-permute-start.15 = (bf16[1216,512]{1,0:T(8,128)(2,1)}, bf16[1216,512]{1,0:T(8,128)(2,1)S(1)}, u32[]{:S(2)}, u32[]{:S(2)}) collective-permute-start(bf16[1216,512]{1,0:T(8,128)(2,1)} %get-tuple-element.104), channel_id=1, source_target_pairs={{0,4},{4,0},{1,5},{5,1},{2,6},{6,2},{3,7},{7,3},{8,12},{12,8},{9,1... | collective-permute-start | bytes 3735560 | tf_op jit(solution)/shard_map/ppermute | solution.py:851
  104.2 1.2 copy-start.3
  105.8 8.9 %collective-permute-start.14 = (bf16[1024,128]{1,0:T(8,128)(2,1)S(1)}, bf16[1024,128]{1,0:T(8,128)(2,1)S(1)}, u32[]{:S(2)}, u32[]{:S(2)}) collective-permute-start(bf16[1024,128]{1,0:T(8,128)(2,1)S(1)} %get-tuple-element.103), channel_id=1, source_target_pairs={{0,1},{1,2},{2,3},{3,0},{4,5},{5,6},{6,7},{7,4},{8,9},{9,10},{10,1... | collective-permute-start | bytes 786440 | tf_op jit(solution)/shard_map/ppermute | solution.py:857
  106.8 13.8 %collective-permute-start.19 = (bf16[1024,128]{1,0:T(8,128)(2,1)S(1)}, bf16[1024,128]{1,0:T(8,128)(2,1)S(1)}, u32[]{:S(2)}, u32[]{:S(2)}) collective-permute-start(bf16[1024,128]{1,0:T(8,128)(2,1)S(1)} %get-tuple-element.117), channel_id=1, source_target_pairs={{0,2},{1,3},{2,0},{3,1},{4,6},{5,7},{6,4},{7,5},{8,10},{9,11},{10,... | collective-permute-start | bytes 786440 | tf_op jit(solution)/shard_map/ppermute | solution.py:857
  108.9 11.7 %collective-permute-start.20 = (bf16[1024,128]{1,0:T(8,128)(2,1)S(1)}, bf16[1024,128]{1,0:T(8,128)(2,1)S(1)}, u32[]{:S(2)}, u32[]{:S(2)}) collective-permute-start(bf16[1024,128]{1,0:T(8,128)(2,1)S(1)} %get-tuple-element.118), channel_id=1, source_target_pairs={{0,3},{1,0},{2,1},{3,2},{4,7},{5,4},{6,5},{7,6},{8,11},{9,8},{10,9... | collective-permute-start | bytes 786440 | tf_op jit(solution)/shard_map/ppermute | solution.py:857
  115.6 20.4 %collective-permute-start.16 = (bf16[256,512]{1,0:T(8,128)(2,1)}, bf16[256,512]{1,0:T(8,128)(2,1)S(1)}, u32[]{:S(2)}, u32[]{:S(2)}) collective-permute-start(bf16[256,512]{1,0:T(8,128)(2,1)} %get-tuple-element.107), channel_id=1, source_target_pairs={{0,24},{8,0},{16,8},{24,16},{1,25},{9,1},{17,9},{25,17},{2,26},{10... | collective-permute-start | bytes 786440 | tf_op jit(solution)/shard_map/ppermute | solution.py:908
  117.9 18.2 %collective-permute-start.17 = (bf16[256,512]{1,0:T(8,128)(2,1)S(1)}, bf16[256,512]{1,0:T(8,128)(2,1)S(1)}, u32[]{:S(2)}, u32[]{:S(2)}) collective-permute-start(bf16[256,512]{1,0:T(8,128)(2,1)S(1)} %get-tuple-element.108), channel_id=1, source_target_pairs={{0,16},{8,24},{16,0},{24,8},{1,17},{9,25},{17,1},{25,9},{2,18},{10... | collective-permute-start | bytes 786440 | tf_op jit(solution)/shard_map/ppermute | solution.py:908
  118.5 17.7 %collective-permute-start.18 = (bf16[256,512]{1,0:T(8,128)(2,1)S(1)}, bf16[256,512]{1,0:T(8,128)(2,1)S(1)}, u32[]{:S(2)}, u32[]{:S(2)}) collective-permute-start(bf16[256,512]{1,0:T(8,128)(2,1)S(1)} %get-tuple-element.109), channel_id=1, source_target_pairs={{0,8},{8,16},{16,24},{24,0},{1,9},{9,17},{17,25},{25,1},{2,10},{10... | collective-permute-start | bytes 786440 | tf_op jit(solution)/shard_map/ppermute | solution.py:908
  124.8 16.5 %all-to-all-start.1 = ((bf16[16,176,128]{2,1,0:T(8,128)(2,1)}), bf16[16,176,128]{2,1,0:T(8,128)(2,1)}, u32[]{:S(2)}, u32[]{:S(2)}) async-start(bf16[16,176,128]{2,1,0:T(8,128)(2,1)} %get-tuple-element.120), calls=%async_computation.1 | async-start | bytes 1441792 | tf_op jit(solution)/shard_map/all_to_all | solution.py:912
  131.5 5.8 %collective-permute-start.21 = (bf16[176,128]{1,0:T(8,128)(2,1)}, bf16[176,128]{1,0:T(8,128)(2,1)}, u32[]{:S(2)}, u32[]{:S(2)}) collective-permute-start(bf16[176,128]{1,0:T(8,128)(2,1)} %get-tuple-element.122), channel_id=1, source_target_pairs={{0,1},{1,2},{2,3},{3,0},{4,5},{5,6},{6,7},{7,4},{8,9},{9,10},{10,1... | collective-permute-start | bytes 135176 | tf_op jit(solution)/shard_map/ppermute | solution.py:857
  133.6 5.0 %collective-permute-start.22 = (bf16[176,128]{1,0:T(8,128)(2,1)}, bf16[176,128]{1,0:T(8,128)(2,1)}, u32[]{:S(2)}, u32[]{:S(2)}) collective-permute-start(bf16[176,128]{1,0:T(8,128)(2,1)} %get-tuple-element.123), channel_id=1, source_target_pairs={{0,2},{1,3},{2,0},{3,1},{4,6},{5,7},{6,4},{7,5},{8,10},{9,11},{10,... | collective-permute-start | bytes 135176 | tf_op jit(solution)/shard_map/ppermute | solution.py:857
  136.0 3.9 %collective-permute-start.23 = (bf16[176,128]{1,0:T(8,128)(2,1)}, bf16[176,128]{1,0:T(8,128)(2,1)}, u32[]{:S(2)}, u32[]{:S(2)}) collective-permute-start(bf16[176,128]{1,0:T(8,128)(2,1)} %get-tuple-element.124), channel_id=1, source_target_pairs={{0,3},{1,0},{2,1},{3,2},{4,7},{5,4},{6,5},{7,6},{8,11},{9,8},{10,9... | collective-permute-start | bytes 135176 | tf_op jit(solution)/shard_map/ppermute | solution.py:857
  137.2 22.7 %copy-start.18 = (bf16[192,512]{1,0:T(8,128)(2,1)}, bf16[192,512]{1,0:T(8,128)(2,1)S(1)}, u32[]{:S(2)}) copy-start(bf16[192,512]{1,0:T(8,128)(2,1)S(1)} %get-tuple-element.132) | copy-start | bytes 589828
  143.6 16.5 %all-to-all-start.2 = ((bf16[16,192,128]{2,1,0:T(8,128)(2,1)}), bf16[16,192,128]{2,1,0:T(8,128)(2,1)S(1)}, u32[]{:S(2)}, u32[]{:S(2)}) async-start(bf16[16,192,128]{2,1,0:T(8,128)(2,1)} %get-tuple-element.128), calls=%async_computation.2 | async-start | bytes 1572864 | tf_op jit(solution)/shard_map/all_to_all | solution.py:916
  149.8 4.5 %collective-permute-start.26 = (bf16[160,128]{1,0:T(8,128)(2,1)S(1)}, bf16[160,128]{1,0:T(8,128)(2,1)S(1)}, u32[]{:S(2)}, u32[]{:S(2)}) collective-permute-start(bf16[160,128]{1,0:T(8,128)(2,1)S(1)} %get-tuple-element.129.d0), channel_id=1, source_target_pairs={{0,3},{1,0},{2,1},{3,2},{4,7},{5,4},{6,5},{7,6},{8,11},{9,8},{10,9... | collective-permute-start | bytes 122888 | tf_op jit(solution)/shard_map/ppermute | solution.py:857
  153.2 4.7 %collective-permute-start.25 = (bf16[160,128]{1,0:T(8,128)(2,1)S(1)}, bf16[160,128]{1,0:T(8,128)(2,1)S(1)}, u32[]{:S(2)}, u32[]{:S(2)}) collective-permute-start(bf16[160,128]{1,0:T(8,128)(2,1)S(1)} %get-tuple-element.129.d0), channel_id=1, source_target_pairs={{0,2},{1,3},{2,0},{3,1},{4,6},{5,7},{6,4},{7,5},{8,10},{9,11},{10,... | collective-permute-start | bytes 122888 | tf_op jit(solution)/shard_map/ppermute | solution.py:857
  153.6 4.7 %collective-permute-start.24 = (bf16[160,128]{1,0:T(8,128)(2,1)S(1)}, bf16[160,128]{1,0:T(8,128)(2,1)S(1)}, u32[]{:S(2)}, u32[]{:S(2)}) collective-permute-start(bf16[160,128]{1,0:T(8,128)(2,1)S(1)} %get-tuple-element.129.d0), channel_id=1, source_target_pairs={{0,1},{1,2},{2,3},{3,0},{4,5},{5,6},{6,7},{7,4},{8,9},{9,10},{10,1... | collective-permute-start | bytes 122888 | tf_op jit(solution)/shard_map/ppermute | solution.py:857
  160.0 51.4 %copy-start.16 = (f32[640]{0:T(1024)S(1)}, f32[640]{0:T(1024)}, u32[]{:S(2)}) copy-start(f32[640]{0:T(1024)} %ga.5) | copy-start | bytes 7684
  160.0 51.4 %copy-start.17 = (s32[1,2]{1,0:T(1,128)S(1)}, s32[1,2]{1,0:T(1,128)}, u32[]{:S(2)}) copy-start(s32[1,2]{1,0:T(1,128)} %lengths.3) | copy-start | bytes 28
  160.1 47.5 %all-to-all-start.3 = ((bf16[16,4,160,128]{3,2,1,0:T(8,128)(2,1)}), bf16[16,4,160,128]{3,2,1,0:T(8,128)(2,1)S(1)}, u32[]{:S(2)}, u32[]{:S(2)}) async-start(bf16[16,4,160,128]{3,2,1,0:T(8,128)(2,1)} %spread.1), calls=%async_computation.3 | async-start | bytes 5242880 | tf_op jit(solution)/shard_map/all_to_all | solution.py:920
  166.7 37.2 %collective-permute-start.29 = (bf16[16,192,128]{2,1,0:T(8,128)(2,1)S(1)}, bf16[16,192,128]{2,1,0:T(8,128)(2,1)S(1)}, u32[]{:S(2)}, u32[]{:S(2)}) collective-permute-start(bf16[16,192,128]{2,1,0:T(8,128)(2,1)S(1)} %all-to-all-done.2.e0_h), channel_id=1, source_target_pairs={{0,3},{1,0},{2,1},{3,2},{4,7},{5,4},{6,5},{7,6},{8,11},{9,8},{10,9... | collective-permute-start | bytes 2359304 | tf_op jit(solution)/shard_map/ppermute | solution.py:857
  169.7 34.2 %collective-permute-start.28 = (bf16[16,192,128]{2,1,0:T(8,128)(2,1)S(1)}, bf16[16,192,128]{2,1,0:T(8,128)(2,1)S(1)}, u32[]{:S(2)}, u32[]{:S(2)}) collective-permute-start(bf16[16,192,128]{2,1,0:T(8,128)(2,1)S(1)} %all-to-all-done.2.e0_h), channel_id=1, source_target_pairs={{0,2},{1,3},{2,0},{3,1},{4,6},{5,7},{6,4},{7,5},{8,10},{9,11},{10,... | collective-permute-start | bytes 2359304 | tf_op jit(solution)/shard_map/ppermute | solution.py:857
  170.0 37.6 %collective-permute-start.27 = (bf16[16,192,128]{2,1,0:T(8,128)(2,1)S(1)}, bf16[16,192,128]{2,1,0:T(8,128)(2,1)}, u32[]{:S(2)}, u32[]{:S(2)}) collective-permute-start(bf16[16,192,128]{2,1,0:T(8,128)(2,1)S(1)} %all-to-all-done.2.e0_h), channel_id=1, source_target_pairs={{0,1},{1,2},{2,3},{3,0},{4,5},{5,6},{6,7},{7,4},{8,9},{9,10},{10,1... | collective-permute-start | bytes 2359304 | tf_op jit(solution)/shard_map/ppermute | solution.py:857
  170.4 32.8 %collective-permute-start.30 = (bf16[192,512]{1,0:T(8,128)(2,1)}, bf16[192,512]{1,0:T(8,128)(2,1)S(1)}, u32[]{:S(2)}, u32[]{:S(2)}) collective-permute-start(bf16[192,512]{1,0:T(8,128)(2,1)} %copy-done.18), channel_id=1, source_target_pairs={{32,0},{64,32},{96,64},{33,1},{65,33},{97,65},{34,2},{66,34},{98,6... | collective-permute-start | bytes 589832 | tf_op jit(solution)/shard_map/ppermute | solution.py:922
  172.5 30.7 %collective-permute-start.31 = (bf16[64,512]{1,0:T(8,128)(2,1)S(1)}, bf16[64,512]{1,0:T(8,128)(2,1)S(1)}, u32[]{:S(2)}, u32[]{:S(2)}) collective-permute-start(bf16[64,512]{1,0:T(8,128)(2,1)S(1)} %get-tuple-element.133), channel_id=1, source_target_pairs={{64,0},{96,32},{65,1},{97,33},{66,2},{98,34},{67,3},{99,35},{68,4}... | collective-permute-start | bytes 196616 | tf_op jit(solution)/shard_map/ppermute | solution.py:923
  207.6 13.1 %collective-permute-start.36 = (bf16[16,4,160,128]{3,2,1,0:T(8,128)(2,1)S(1)}, bf16[16,4,160,128]{3,2,1,0:T(8,128)(2,1)S(1)}, u32[]{:S(2)}, u32[]{:S(2)}) collective-permute-start(bf16[16,4,160,128]{3,2,1,0:T(8,128)(2,1)S(1)} %all-to-all-done.3.f_h), channel_id=1, source_target_pairs={{0,4},{4,0},{1,5},{5,1},{2,6},{6,2},{3,7},{7,3},{8,12},{12,8},{9,1... | collective-permute-start | bytes 7864328 | tf_op jit(solution)/shard_map/ppermute | solution.py:851
  210.4 10.2 %collective-permute-start.32 = (bf16[16,192,128]{2,1,0:T(8,128)(2,1)S(1)}, bf16[16,192,128]{2,1,0:T(8,128)(2,1)S(1)}, u32[]{:S(2)}, u32[]{:S(2)}) collective-permute-start(bf16[16,192,128]{2,1,0:T(8,128)(2,1)S(1)} %all-to-all-done.2.e0_h), channel_id=1, source_target_pairs={{0,4},{4,0},{1,5},{5,1},{2,6},{6,2},{3,7},{7,3},{8,12},{12,8},{9,1... | collective-permute-start | bytes 2359304 | tf_op jit(solution)/shard_map/ppermute | solution.py:851
  210.4 10.2 %collective-permute-start.33 = (bf16[16,192,128]{2,1,0:T(8,128)(2,1)}, bf16[16,192,128]{2,1,0:T(8,128)(2,1)S(1)}, u32[]{:S(2)}, u32[]{:S(2)}) collective-permute-start(bf16[16,192,128]{2,1,0:T(8,128)(2,1)} %collective-permute-done.27.e1_h), channel_id=1, source_target_pairs={{0,4},{4,0},{1,5},{5,1},{2,6},{6,2},{3,7},{7,3},{8,12},{12,8},{9,1... | collective-permute-start | bytes 2359304 | tf_op jit(solution)/shard_map/ppermute | solution.py:851
  210.9 9.7 %collective-permute-start.34 = (bf16[16,192,128]{2,1,0:T(8,128)(2,1)}, bf16[16,192,128]{2,1,0:T(8,128)(2,1)S(1)}, u32[]{:S(2)}, u32[]{:S(2)}) collective-permute-start(bf16[16,192,128]{2,1,0:T(8,128)(2,1)} %copy-done.6), channel_id=1, source_target_pairs={{0,4},{4,0},{1,5},{5,1},{2,6},{6,2},{3,7},{7,3},{8,12},{12,8},{9,1... | collective-permute-start | bytes 2359304 | tf_op jit(solution)/shard_map/ppermute | solution.py:851
  211.0 9.7 %collective-permute-start.35 = (bf16[16,192,128]{2,1,0:T(8,128)(2,1)}, bf16[16,192,128]{2,1,0:T(8,128)(2,1)S(1)}, u32[]{:S(2)}, u32[]{:S(2)}) collective-permute-start(bf16[16,192,128]{2,1,0:T(8,128)(2,1)} %copy-done.4), channel_id=1, source_target_pairs={{0,4},{4,0},{1,5},{5,1},{2,6},{6,2},{3,7},{7,3},{8,12},{12,8},{9,1... | collective-permute-start | bytes 2359304 | tf_op jit(solution)/shard_map/ppermute | solution.py:851
  211.4 0.9 copy-start.1
  212.3 1.0 copy-start.8
  213.4 1.0 copy-start.9
  214.4 1.0 copy-start.11
  215.4 1.0 copy-start.12
  216.4 1.0 copy-start.13
  217.3 0.9 copy-start.15
  218.3 2.4 %copy-start.5 = (bf16[16,192,128]{2,1,0:T(8,128)(2,1)S(1)}, bf16[16,192,128]{2,1,0:T(8,128)(2,1)}, u32[]{:S(2)}) copy-start(bf16[16,192,128]{2,1,0:T(8,128)(2,1)} %copy-done.4) | copy-start | bytes 2359300
  218.3 2.4 %copy-start.7 = (bf16[16,192,128]{2,1,0:T(8,128)(2,1)S(1)}, bf16[16,192,128]{2,1,0:T(8,128)(2,1)}, u32[]{:S(2)}) copy-start(bf16[16,192,128]{2,1,0:T(8,128)(2,1)} %copy-done.6) | copy-start | bytes 2359300
  (6 other events, 4.6 us)
where the time goes:
time: 232 us; the launch traced here: 231 us
  starting transfers between devices  82.3 us (35%)
  waiting for transfers between devices  66.4 us (29%)
  Pallas kernels  64 us (28%)
  local copies, waits for them, and re-layouts  15.3 us (7%)
    ppermute x1, waiting for transfers between devices, shards(): lax.ppermute(for_far_back, 'x', [(i + 2, i) for i in range(2)])  29.4 us
    ppermute x15, starting transfers between devices, gather_dp(): lax.ppermute(pieces[step], 'dp', [(i, (i + step) % DP) for i in range(DP)])  21.8 us
    pallas_call x1, Pallas kernels, run_forward(): pl.pallas_call(forward_kernel, in_specs=[SMEM] + [VMEM] * 3 + [ANY] * 16,...  21.7 us
    ppermute x15, waiting for transfers between devices, gather_dp(): lax.ppermute(pieces[step], 'dp', [(i, (i + step) % DP) for i in range(DP)])  18.9 us
    ppermute x12, starting transfers between devices, swap_cores(): return lax.ppermute(array, 'core', [(0, 1), (1, 0)])  17.5 us
    pallas_call x1, Pallas kernels, run_backward(): pl.pallas_call(backward_kernel, in_specs=[VMEM] * 2 + [ANY] * 8, out_spec...  14.7 us
    unnamed x59, local copies, waits for them, and re-layouts  14.3 us
    pallas_call x1, Pallas kernels, run_unpack(): pl.pallas_call(unpack_kernel, in_specs=[ANY] * 10, out_specs=[VMEM] * 2 +...  10.2 us
  transfers between devices with their start and end apart: 41, of which 18 were waited for; matrix products, arithmetic and copies ran while one was open for 0% of the time, Pallas kernels for 11%

commit v1 on v0

--- a/solution.py
+++ b/solution.py
@@ -43,7 +43,7 @@
 A_GATE, A_UP, A_DOWN, A_PROJ, A_GAIN, A_ROWS = 0, 5120, 10240, 15360, 17920, 18432
 B_QUERY, B_KV, B_GAIN, B_ROWS = 0, 2560, 3840, 4096
 DP = 4
-A_DP = 7168
+A_DP = 6144
 A_XZ = A_ROWS - A_DP
 A_DP_PIECE, B_PIECE, A_XZ_PIECE = A_DP // DP, B_ROWS // DP, A_XZ // CHIPS
 A_DP_BLOCK, B_BLOCK, A_XZ_BLOCK = A_DP_PIECE // CHIPS, B_PIECE // CHIPS, A_XZ_PIECE // DP

time: 232 us -> 234 us (level)
  starting transfers between devices: 82.3 us -> 87.9 us
  waiting for transfers between devices: 66.4 us -> 61.3 us
    ppermute x15, waiting for transfers between devices: 18.9 us -> 12.7 us  [gather_dp(): lax.ppermute(pieces[step], 'dp', [(i, (i + step) % DP) for i in range(DP)])]
    all_to_all x1, starting transfers between devices: 6.68 us -> 10.1 us  [shards(): first = lax.all_to_all(first, CHIP, 0, 0, tiled=True)]
    ppermute x12, starting transfers between devices: 17.5 us -> 20.8 us  [swap_cores(): return lax.ppermute(array, 'core', [(0, 1), (1, 0)])]
    unnamed x59 -> x65, local copies, waits for them, and re-layouts: 14.3 us -> 16.2 us
  transfers between devices with their start and end apart: 41 -> 41, of which waited for: 18 -> 15; matrix products, arithmetic and copies ran while one was open for 0% -> 0% of each run, Pallas kernels for 11% -> 10%
where the time goes in v1:
time: 234 us; the launch traced here: 233 us
  starting transfers between devices  87.9 us (38%)
  Pallas kernels  63.5 us (27%)
  waiting for transfers between devices  61.3 us (26%)
  local copies, waits for them, and re-layouts  17.1 us (7%)
    ppermute x1, waiting for transfers between devices, shards(): lax.ppermute(for_far_back, 'x', [(i + 2, i) for i in range(2)])  31.4 us
    pallas_call x1, Pallas kernels, run_forward(): pl.pallas_call(forward_kernel, in_specs=[SMEM] + [VMEM] * 3 + [ANY] * 16,...  21.7 us
    ppermute x12, starting transfers between devices, swap_cores(): return lax.ppermute(array, 'core', [(0, 1), (1, 0)])  20.8 us
    ppermute x15, starting transfers between devices, gather_dp(): lax.ppermute(pieces[step], 'dp', [(i, (i + step) % DP) for i in range(DP)])  20.2 us
    unnamed x65, local copies, waits for them, and re-layouts  16.2 us
    pallas_call x1, Pallas kernels, run_backward(): pl.pallas_call(backward_kernel, in_specs=[VMEM] * 2 + [ANY] * 8, out_spec...  14.7 us
    ppermute x15, waiting for transfers between devices, gather_dp(): lax.ppermute(pieces[step], 'dp', [(i, (i + step) % DP) for i in range(DP)])  12.7 us
    pallas_call x1, Pallas kernels, run_unpack(): pl.pallas_call(unpack_kernel, in_specs=[ANY] * 10, out_specs=[VMEM] * 2 +...  10.5 us
  transfers between devices with their start and end apart: 41, of which 15 were waited for; matrix products, arithmetic and copies ran while one was open for 0% of the time, Pallas kernels for 10%

profile of v1, /device:TPU:3, one launch (start us, length us, event | category | flops | bytes accessed | tf_op | source)
XLA Modules:
  0.0 232.9 jit_solution(12963411952755775788)
XLA Ops:
  0.7 3.3 %collective-permute-start = (bf16[192,640]{1,0:T(8,128)(2,1)}, bf16[192,640]{1,0:T(8,128)(2,1)S(1)}, u32[]{:S(2)}, u32[]{:S(2)}) collective-permute-start(bf16[192,640]{1,0:T(8,128)(2,1)} %bitcast.9), channel_id=1, source_target_pairs={{0,32},{32,64},{64,96},{1,33},{33,65},{65,97},{2,34},{34,66},{66,9... | collective-permute-start | bytes 737288 | tf_op jit(solution)/shard_map/ppermute | solution.py:873
  4.6 0.9 dynamic-slice_bitcast_fusion
  5.5 1.9 collective-permute-start.1
  7.4 2.3 collective-permute-done
  9.8 1.1 broadcast_select_fusion
  10.9 3.8 %collective-permute-start.4 = (bf16[256,640]{1,0:T(8,128)(2,1)S(1)}, bf16[256,640]{1,0:T(8,128)(2,1)S(1)}, u32[]{:S(2)}, u32[]{:S(2)}) collective-permute-start(bf16[256,640]{1,0:T(8,128)(2,1)S(1)} %get-tuple-element.152), channel_id=1, source_target_pairs={{0,24},{8,0},{16,8},{24,16},{1,25},{9,1},{17,9},{25,17},{2,26},{10... | collective-permute-start | bytes 983048 | tf_op jit(solution)/shard_map/ppermute | solution.py:879
  14.7 0.7 collective-permute-start.2
  15.5 2.5 %collective-permute-start.5 = (bf16[448,640]{1,0:T(8,128)(2,1)S(1)}, bf16[448,640]{1,0:T(8,128)(2,1)S(1)}, u32[]{:S(2)}, u32[]{:S(2)}) collective-permute-start(bf16[448,640]{1,0:T(8,128)(2,1)S(1)} %pad_maximum_fusion.w0_h), channel_id=1, source_target_pairs={{0,4},{4,0},{1,5},{5,1},{2,6},{6,2},{3,7},{7,3},{8,12},{12,8},{9,1... | collective-permute-start | bytes 1720328 | tf_op jit(solution)/shard_map/ppermute | solution.py:851
  18.0 3.9 %collective-permute-done.4.w3_h = bf16[256,640]{1,0:T(8,128)(2,1)S(1)} collective-permute-done((bf16[256,640]{1,0:T(8,128)(2,1)S(1)}, bf16[256,640]{1,0:T(8,128)(2,1)S(1)}, u32[]{:S(2)}, u32[]{:S(2)}) %collective-permute-start.4) | collective-permute-done | bytes 327712 | tf_op jit(solution)/shard_map/ppermute | solution.py:879
  21.9 7.8 %collective-permute-start.8 = (bf16[256,640]{1,0:T(8,128)(2,1)S(1)}, bf16[256,640]{1,0:T(8,128)(2,1)S(1)}, u32[]{:S(2)}, u32[]{:S(2)}) collective-permute-start(bf16[256,640]{1,0:T(8,128)(2,1)S(1)} %collective-permute-done.4.w3_h), channel_id=1, source_target_pairs={{0,4},{4,0},{1,5},{5,1},{2,6},{6,2},{3,7},{7,3},{8,12},{12,8},{9,1... | collective-permute-start | bytes 983048 | tf_op jit(solution)/shard_map/ppermute | solution.py:851
  29.8 2.5 %collective-permute-done.2.w1_h = bf16[256,640]{1,0:T(8,128)(2,1)S(1)} collective-permute-done((bf16[256,640]{1,0:T(8,128)(2,1)S(1)}, bf16[256,640]{1,0:T(8,128)(2,1)S(1)}, u32[]{:S(2)}, u32[]{:S(2)}) %collective-permute-start.2) | collective-permute-done | bytes 327712 | tf_op jit(solution)/shard_map/ppermute | solution.py:879
  32.2 0.9 collective-permute-start.6
  33.1 1.2 collective-permute-done.6.w5_h
  35.1 21.7 %forward.1 = (f32[1,640]{1,0:T(1,128)}, bf16[768,256]{1,0:T(8,128)(2,1)}, bf16[2432,256]{1,0:T(8,128)(2,1)}, bf16[2432,256]{1,0:T(8,128)(2,1)}, bf16[768,256]{1,...) custom-call(s32[1,2]{1,0:T(1,128)} %lengths.3, ...), custom_call_target="tpu_custom_call" | custom-call | flops 8000000000 | bytes 30000000 | tf_op jit(solution)/shard_map/forward/pallas_call | solution.py:670
  57.4 4.0 %collective-permute-done.9.recv_h = bf16[192,5504]{1,0:T(8,128)(2,1)S(1)} collective-permute-done((bf16[192,5504]{1,0:T(8,128)(2,1)}, bf16[192,5504]{1,0:T(8,128)(2,1)S(1)}, u32[]{:S(2)}, u32[]{:S(2)}) %collective-permute-start.9) | collective-permute-done | bytes 2113568 | tf_op jit(solution)/shard_map/ppermute | solution.py:851
  61.5 1.6 copy-done.22
  63.7 5.4 %halves.1 = (bf16[1536,128]{1,0:T(8,128)(2,1)S(1)}, bf16[1536,128]{1,0:T(8,128)(2,1)}, bf16[1536,128]{1,0:T(8,128)(2,1)}, bf16[1536,128]{1,0:T(8,128)(2,1)}, bf16[16,768,128]{2,1,0:T(8,128)(2,1)}) custom-call(f32[1,640]{1,0:T(1,128)S(1)} %copy-done.23, bf16[192,5504]{1,0:T(8,128)(2,1)S(1)} %copy-done.22, bf16[192,5504]{1,0:T(8,128)(2,1)S(1)} %collective-permute-done.9.recv_h), custom_call_target="tpu_custom_call" | custom-call | flops 2000000000 | bytes 10000000 | tf_op jit(solution)/shard_map/halves/pallas_call | solution.py:723
  69.1 7.0 %all-to-all-start = ((bf16[16,768,128]{2,1,0:T(8,128)(2,1)}), bf16[16,768,128]{2,1,0:T(8,128)(2,1)}, u32[]{:S(2)}, u32[]{:S(2)}) async-start(bf16[16,768,128]{2,1,0:T(8,128)(2,1)} %get-tuple-element.119), calls=%async_computation | async-start | bytes 6291456 | tf_op jit(solution)/shard_map/all_to_all | solution.py:895
  76.1 1.3 collective-permute-start.10
  77.4 2.6 %collective-permute-start.11 = (bf16[1536,128]{1,0:T(8,128)(2,1)}, bf16[1536,128]{1,0:T(8,128)(2,1)}, u32[]{:S(2)}, u32[]{:S(2)}) collective-permute-start(bf16[1536,128]{1,0:T(8,128)(2,1)} %get-tuple-element.99), channel_id=1, source_target_pairs={{0,2},{1,3},{2,0},{3,1},{4,6},{5,7},{6,4},{7,5},{8,10},{9,11},{10,... | collective-permute-start | bytes 1179656 | tf_op jit(solution)/shard_map/ppermute | solution.py:857
  80.0 1.1 collective-permute-start.12
  81.1 14.7 %backward.1 = (bf16[1216,512]{1,0:T(8,128)(2,1)}, bf16[1216,512]{1,0:T(8,128)(2,1)}, f32[192,640]{1,0:T(8,128)}, bf16[4096,128]{1,0:T(8,128)(2,1)}, bf16[4096,128]{1,0:T(8,128)(2,1)}) custom-call(f32[4,64,128]{2,1,0:T(8,128)} %constant.28.clone.tables, f32[640]{0:T(1024)} %ga.5, bf16[768,256]{1,0:T(8,128)(2,1)} %get-tuple-element.89.q_h, ...), custom_call_target="tpu_custom_call" | custom-call | flops 999999995904 | bytes 1000000000 | tf_op jit(solution)/shard_map/backward/pallas_call | solution.py:698
  95.8 1.2 collective-permute-done.11.a2
  97.0 1.8 collective-permute-start.13
  98.8 2.5 %collective-permute-done.13.recv = bf16[4096,128]{1,0:T(8,128)(2,1)S(1)} collective-permute-done((bf16[4096,128]{1,0:T(8,128)(2,1)}, bf16[4096,128]{1,0:T(8,128)(2,1)S(1)}, u32[]{:S(2)}, u32[]{:S(2)}) %collective-permute-start.13) | collective-permute-done | bytes 1048608 | tf_op jit(solution)/shard_map/ppermute | solution.py:851
  101.3 1.2 copy-done.3
  102.9 1.0 collective-permute-start.14
  104.0 2.1 collective-permute-start.19
  106.1 1.3 collective-permute-start.20
  107.4 4.4 %collective-permute-done.14.b1 = bf16[1024,128]{1,0:T(8,128)(2,1)S(1)} collective-permute-done((bf16[1024,128]{1,0:T(8,128)(2,1)S(1)}, bf16[1024,128]{1,0:T(8,128)(2,1)S(1)}, u32[]{:S(2)}, u32[]{:S(2)}) %collective-permute-start.14) | collective-permute-done | bytes 262176 | tf_op jit(solution)/shard_map/ppermute | solution.py:857
  112.0 2.6 %collective-permute-start.16 = (bf16[256,512]{1,0:T(8,128)(2,1)S(1)}, bf16[256,512]{1,0:T(8,128)(2,1)S(1)}, u32[]{:S(2)}, u32[]{:S(2)}) collective-permute-start(bf16[256,512]{1,0:T(8,128)(2,1)S(1)} %get-tuple-element.107), channel_id=1, source_target_pairs={{0,24},{8,0},{16,8},{24,16},{1,25},{9,1},{17,9},{25,17},{2,26},{10... | collective-permute-start | bytes 786440 | tf_op jit(solution)/shard_map/ppermute | solution.py:908
  115.8 2.1 collective-permute-done.19.b2
  117.8 4.1 %first_sum.1 = (bf16[16,160,128]{2,1,0:T(8,128)(2,1)}, bf16[192,128]{1,0:T(8,128)(2,1)S(1)}, bf16[192,128]{1,0:T(8,128)(2,1)S(1)}, bf16[192,128]{1,0:T(8,128)(2,1)S(1)}, bf16[192,128]{1,0:T(8,128)(2,1)S(1)}) custom-call(bf16[1536,128]{1,0:T(8,128)(2,1)S(1)} %get-tuple-element.111.a0, bf16[1536,128]{1,0:T(8,128)(2,1)} %collective-permute-done.10.a1, ...), custom_call_target="tpu_custom_call" | custom-call | flops 1000000 | bytes 8000000 | tf_op jit(solution)/shard_map/first_sum/pallas_call | solution.py:752
  123.8 10.1 %all-to-all-start.1 = ((bf16[16,160,128]{2,1,0:T(8,128)(2,1)}), bf16[16,160,128]{2,1,0:T(8,128)(2,1)}, u32[]{:S(2)}, u32[]{:S(2)}) async-start(bf16[16,160,128]{2,1,0:T(8,128)(2,1)} %get-tuple-element.120), calls=%async_computation.1 | async-start | bytes 1310720 | tf_op jit(solution)/shard_map/all_to_all | solution.py:912
  133.9 1.3 collective-permute-start.21
  135.2 2.6 %collective-permute-start.22 = (bf16[192,128]{1,0:T(8,128)(2,1)}, bf16[192,128]{1,0:T(8,128)(2,1)}, u32[]{:S(2)}, u32[]{:S(2)}) collective-permute-start(bf16[192,128]{1,0:T(8,128)(2,1)} %copy-done.20), channel_id=1, source_target_pairs={{0,2},{1,3},{2,0},{3,1},{4,6},{5,7},{6,4},{7,5},{8,10},{9,11},{10,... | collective-permute-start | bytes 147464 | tf_op jit(solution)/shard_map/ppermute | solution.py:857
  137.8 1.1 collective-permute-start.23
  139.3 0.7 copy-done.10
  140.1 1.2 collective-permute-done.23.c3
  141.4 0.7 all-to-all-done.1.xz
  142.1 2.2 second_sum.1
  144.3 6.0 %all-to-all-start.2 = ((bf16[16,192,128]{2,1,0:T(8,128)(2,1)}), bf16[16,192,128]{2,1,0:T(8,128)(2,1)S(1)}, u32[]{:S(2)}, u32[]{:S(2)}) async-start(bf16[16,192,128]{2,1,0:T(8,128)(2,1)} %get-tuple-element.128), calls=%async_computation.2 | async-start | bytes 1572864 | tf_op jit(solution)/shard_map/all_to_all | solution.py:916
  150.4 2.7 %collective-permute-start.26 = (bf16[160,128]{1,0:T(8,128)(2,1)S(1)}, bf16[160,128]{1,0:T(8,128)(2,1)S(1)}, u32[]{:S(2)}, u32[]{:S(2)}) collective-permute-start(bf16[160,128]{1,0:T(8,128)(2,1)S(1)} %get-tuple-element.129.d0), channel_id=1, source_target_pairs={{0,3},{1,0},{2,1},{3,2},{4,7},{5,4},{6,5},{7,6},{8,11},{9,8},{10,9... | collective-permute-start | bytes 122888 | tf_op jit(solution)/shard_map/ppermute | solution.py:857
  153.4 0.8 collective-permute-start.24
  154.2 3.4 %collective-permute-done.25.d2 = bf16[160,128]{1,0:T(8,128)(2,1)S(1)} collective-permute-done((bf16[160,128]{1,0:T(8,128)(2,1)S(1)}, bf16[160,128]{1,0:T(8,128)(2,1)S(1)}, u32[]{:S(2)}, u32[]{:S(2)}) %collective-permute-start.25) | collective-permute-done | bytes 40992 | tf_op jit(solution)/shard_map/ppermute | solution.py:857
  157.9 1.6 spread.1
  159.6 7.0 %all-to-all-start.3 = ((bf16[16,4,160,128]{3,2,1,0:T(8,128)(2,1)}), bf16[16,4,160,128]{3,2,1,0:T(8,128)(2,1)S(1)}, u32[]{:S(2)}, u32[]{:S(2)}) async-start(bf16[16,4,160,128]{3,2,1,0:T(8,128)(2,1)} %spread.1), calls=%async_computation.3 | async-start | bytes 5242880 | tf_op jit(solution)/shard_map/all_to_all | solution.py:920
  166.6 0.7 collective-permute-start.29
  167.8 0.8 collective-permute-start.27
  168.6 2.1 collective-permute-start.30
  170.7 1.3 collective-permute-start.31
  172.0 31.4 %collective-permute-done.31.far_back = bf16[64,512]{1,0:T(8,128)(2,1)S(1)} collective-permute-done((bf16[64,512]{1,0:T(8,128)(2,1)S(1)}, bf16[64,512]{1,0:T(8,128)(2,1)S(1)}, u32[]{:S(2)}, u32[]{:S(2)}) %collective-permute-start.31) | collective-permute-done | bytes 65568 | tf_op jit(solution)/shard_map/ppermute | solution.py:923
  204.0 0.9 copy-done.4
  204.9 0.9 copy-done.6
  205.8 6.1 %collective-permute-start.36 = (bf16[16,4,160,128]{3,2,1,0:T(8,128)(2,1)S(1)}, bf16[16,4,160,128]{3,2,1,0:T(8,128)(2,1)S(1)}, u32[]{:S(2)}, u32[]{:S(2)}) collective-permute-start(bf16[16,4,160,128]{3,2,1,0:T(8,128)(2,1)S(1)} %all-to-all-done.3.f_h), channel_id=1, source_target_pairs={{0,4},{4,0},{1,5},{5,1},{2,6},{6,2},{3,7},{7,3},{8,12},{12,8},{9,1... | collective-permute-start | bytes 7864328 | tf_op jit(solution)/shard_map/ppermute | solution.py:851
  212.9 0.9 copy-done.1
  213.9 1.0 copy-done.8
  214.9 1.0 copy-done.9
  215.9 1.0 copy-done.11
  216.9 1.0 copy-done.12
  217.9 1.0 copy-done.13
  218.9 0.9 copy-done.15
  219.8 2.3 token_grad.1
  222.2 10.5 %unpack.1 = (f32[640]{0:T(1024)}, f32[640]{0:T(1024)}, f32[640,2048]{1,0:T(8,128)}, f32[640,2048]{1,0:T(8,128)}, f32[2048,640]{1,0:T(8,128)}, /*index=5*/f32[102...) custom-call(bf16[16,192,128]{2,1,0:T(8,128)(2,1)S(1)} %all-to-all-done.2.e0_h, ...), custom_call_target="tpu_custom_call" | custom-call | bytes 30000000 | tf_op jit(solution)/shard_map/unpack/pallas_call | solution.py:791
  (99 shorter events, 9.3 us)
Async XLA Ops:
  0.6 14.8 %copy-start = (bf16[1,192,640]{2,1,0:T(8,128)(2,1)S(1)}, bf16[1,192,640]{2,1,0:T(8,128)(2,1)}, u32[]{:S(2)}) copy-start(bf16[1,192,640]{2,1,0:T(8,128)(2,1)} %param.13) | copy-start | bytes 737284
  0.7 9.1 %collective-permute-start = (bf16[192,640]{1,0:T(8,128)(2,1)}, bf16[192,640]{1,0:T(8,128)(2,1)S(1)}, u32[]{:S(2)}, u32[]{:S(2)}) collective-permute-start(bf16[192,640]{1,0:T(8,128)(2,1)} %bitcast.9), channel_id=1, source_target_pairs={{0,32},{32,64},{64,96},{1,33},{33,65},{65,97},{2,34},{34,66},{66,9... | collective-permute-start | bytes 737288 | tf_op jit(solution)/shard_map/ppermute | solution.py:873
  5.5 4.3 %collective-permute-start.1 = (bf16[64,640]{1,0:T(8,128)(2,1)S(1)}, bf16[64,640]{1,0:T(8,128)(2,1)S(1)}, u32[]{:S(2)}, u32[]{:S(2)}) collective-permute-start(bf16[64,640]{1,0:T(8,128)(2,1)S(1)} %dynamic-slice_bitcast_fusion), channel_id=1, source_target_pairs={{0,64},{32,96},{1,65},{33,97},{2,66},{34,98},{3,67},{35,99},{4,68}... | collective-permute-start | bytes 245768 | tf_op jit(solution)/shard_map/ppermute | solution.py:874
  10.9 11.0 %collective-permute-start.4 = (bf16[256,640]{1,0:T(8,128)(2,1)S(1)}, bf16[256,640]{1,0:T(8,128)(2,1)S(1)}, u32[]{:S(2)}, u32[]{:S(2)}) collective-permute-start(bf16[256,640]{1,0:T(8,128)(2,1)S(1)} %get-tuple-element.152), channel_id=1, source_target_pairs={{0,24},{8,0},{16,8},{24,16},{1,25},{9,1},{17,9},{25,17},{2,26},{10... | collective-permute-start | bytes 983048 | tf_op jit(solution)/shard_map/ppermute | solution.py:879
  14.7 15.0 %collective-permute-start.3 = (bf16[256,640]{1,0:T(8,128)(2,1)S(1)}, bf16[256,640]{1,0:T(8,128)(2,1)S(1)}, u32[]{:S(2)}, u32[]{:S(2)}) collective-permute-start(bf16[256,640]{1,0:T(8,128)(2,1)S(1)} %get-tuple-element.153), channel_id=1, source_target_pairs={{0,16},{8,24},{16,0},{24,8},{1,17},{9,25},{17,1},{25,9},{2,18},{10... | collective-permute-start | bytes 983048 | tf_op jit(solution)/shard_map/ppermute | solution.py:879
  14.7 17.5 %collective-permute-start.2 = (bf16[256,640]{1,0:T(8,128)(2,1)S(1)}, bf16[256,640]{1,0:T(8,128)(2,1)S(1)}, u32[]{:S(2)}, u32[]{:S(2)}) collective-permute-start(bf16[256,640]{1,0:T(8,128)(2,1)S(1)} %get-tuple-element.154), channel_id=1, source_target_pairs={{0,8},{8,16},{16,24},{24,0},{1,9},{9,17},{17,25},{25,1},{2,10},{10... | collective-permute-start | bytes 983048 | tf_op jit(solution)/shard_map/ppermute | solution.py:879
  15.5 18.9 %copy-start.24 = (bf16[448,640]{1,0:T(8,128)(2,1)}, bf16[448,640]{1,0:T(8,128)(2,1)S(1)}, u32[]{:S(2)}) copy-start(bf16[448,640]{1,0:T(8,128)(2,1)S(1)} %pad_maximum_fusion.w0_h) | copy-start | bytes 1720324
  15.5 17.6 %collective-permute-start.5 = (bf16[448,640]{1,0:T(8,128)(2,1)S(1)}, bf16[448,640]{1,0:T(8,128)(2,1)S(1)}, u32[]{:S(2)}, u32[]{:S(2)}) collective-permute-start(bf16[448,640]{1,0:T(8,128)(2,1)S(1)} %pad_maximum_fusion.w0_h), channel_id=1, source_target_pairs={{0,4},{4,0},{1,5},{5,1},{2,6},{6,2},{3,7},{7,3},{8,12},{12,8},{9,1... | collective-permute-start | bytes 1720328 | tf_op jit(solution)/shard_map/ppermute | solution.py:851
  21.9 12.4 %copy-start.26 = (bf16[256,640]{1,0:T(8,128)(2,1)}, bf16[256,640]{1,0:T(8,128)(2,1)S(1)}, u32[]{:S(2)}) copy-start(bf16[256,640]{1,0:T(8,128)(2,1)S(1)} %collective-permute-done.4.w3_h) | copy-start | bytes 983044
  21.9 11.2 %collective-permute-start.8 = (bf16[256,640]{1,0:T(8,128)(2,1)S(1)}, bf16[256,640]{1,0:T(8,128)(2,1)S(1)}, u32[]{:S(2)}, u32[]{:S(2)}) collective-permute-start(bf16[256,640]{1,0:T(8,128)(2,1)S(1)} %collective-permute-done.4.w3_h), channel_id=1, source_target_pairs={{0,4},{4,0},{1,5},{5,1},{2,6},{6,2},{3,7},{7,3},{8,12},{12,8},{9,1... | collective-permute-start | bytes 983048 | tf_op jit(solution)/shard_map/ppermute | solution.py:851
  29.7 4.7 %copy-start.27 = (bf16[256,640]{1,0:T(8,128)(2,1)}, bf16[256,640]{1,0:T(8,128)(2,1)S(1)}, u32[]{:S(2)}) copy-start(bf16[256,640]{1,0:T(8,128)(2,1)S(1)} %collective-permute-done.3.w2_h) | copy-start | bytes 983044
  29.7 3.4 %collective-permute-start.7 = (bf16[256,640]{1,0:T(8,128)(2,1)S(1)}, bf16[256,640]{1,0:T(8,128)(2,1)S(1)}, u32[]{:S(2)}, u32[]{:S(2)}) collective-permute-start(bf16[256,640]{1,0:T(8,128)(2,1)S(1)} %collective-permute-done.3.w2_h), channel_id=1, source_target_pairs={{0,4},{4,0},{1,5},{5,1},{2,6},{6,2},{3,7},{7,3},{8,12},{12,8},{9,1... | collective-permute-start | bytes 983048 | tf_op jit(solution)/shard_map/ppermute | solution.py:851
  32.2 2.1 copy-start.28
  32.2 2.1 collective-permute-start.6
  33.1 1.3 copy-start.25
  33.1 1.3 copy-start.29
  33.1 1.3 copy-start.30
  56.8 4.7 %collective-permute-start.9 = (bf16[192,5504]{1,0:T(8,128)(2,1)}, bf16[192,5504]{1,0:T(8,128)(2,1)S(1)}, u32[]{:S(2)}, u32[]{:S(2)}) collective-permute-start(bf16[192,5504]{1,0:T(8,128)(2,1)} %get-tuple-element.87), channel_id=1, source_target_pairs={{0,4},{4,0},{1,5},{5,1},{2,6},{6,2},{3,7},{7,3},{8,12},{12,8},{9,1... | collective-permute-start | bytes 6340616 | tf_op jit(solution)/shard_map/ppermute | solution.py:851
  61.5 1.6 copy-start.22
  69.1 48.8 %all-to-all-start = ((bf16[16,768,128]{2,1,0:T(8,128)(2,1)}), bf16[16,768,128]{2,1,0:T(8,128)(2,1)}, u32[]{:S(2)}, u32[]{:S(2)}) async-start(bf16[16,768,128]{2,1,0:T(8,128)(2,1)} %get-tuple-element.119), calls=%async_computation | async-start | bytes 6291456 | tf_op jit(solution)/shard_map/all_to_all | solution.py:895
  76.1 19.7 %collective-permute-start.10 = (bf16[1536,128]{1,0:T(8,128)(2,1)}, bf16[1536,128]{1,0:T(8,128)(2,1)}, u32[]{:S(2)}, u32[]{:S(2)}) collective-permute-start(bf16[1536,128]{1,0:T(8,128)(2,1)} %get-tuple-element.98), channel_id=1, source_target_pairs={{0,1},{1,2},{2,3},{3,0},{4,5},{5,6},{6,7},{7,4},{8,9},{9,10},{10,1... | collective-permute-start | bytes 1179656 | tf_op jit(solution)/shard_map/ppermute | solution.py:857
  77.4 19.6 %collective-permute-start.11 = (bf16[1536,128]{1,0:T(8,128)(2,1)}, bf16[1536,128]{1,0:T(8,128)(2,1)}, u32[]{:S(2)}, u32[]{:S(2)}) collective-permute-start(bf16[1536,128]{1,0:T(8,128)(2,1)} %get-tuple-element.99), channel_id=1, source_target_pairs={{0,2},{1,3},{2,0},{3,1},{4,6},{5,7},{6,4},{7,5},{8,10},{9,11},{10,... | collective-permute-start | bytes 1179656 | tf_op jit(solution)/shard_map/ppermute | solution.py:857
  80.0 17.0 %collective-permute-start.12 = (bf16[1536,128]{1,0:T(8,128)(2,1)}, bf16[1536,128]{1,0:T(8,128)(2,1)}, u32[]{:S(2)}, u32[]{:S(2)}) collective-permute-start(bf16[1536,128]{1,0:T(8,128)(2,1)} %get-tuple-element.100), channel_id=1, source_target_pairs={{0,3},{1,0},{2,1},{3,2},{4,7},{5,4},{6,5},{7,6},{8,11},{9,8},{10,9... | collective-permute-start | bytes 1179656 | tf_op jit(solution)/shard_map/ppermute | solution.py:857
  95.8 15.9 %copy-start.2 = (bf16[1216,512]{1,0:T(8,128)(2,1)S(1)}, bf16[1216,512]{1,0:T(8,128)(2,1)}, u32[]{:S(2)}) copy-start(bf16[1216,512]{1,0:T(8,128)(2,1)} %get-tuple-element.94.mine) | copy-start | bytes 3735556
  97.0 4.3 %collective-permute-start.13 = (bf16[4096,128]{1,0:T(8,128)(2,1)}, bf16[4096,128]{1,0:T(8,128)(2,1)S(1)}, u32[]{:S(2)}, u32[]{:S(2)}) collective-permute-start(bf16[4096,128]{1,0:T(8,128)(2,1)} %get-tuple-element.102), channel_id=1, source_target_pairs={{0,4},{4,0},{1,5},{5,1},{2,6},{6,2},{3,7},{7,3},{8,12},{12,8},{9,1... | collective-permute-start | bytes 3145736 | tf_op jit(solution)/shard_map/ppermute | solution.py:851
  98.8 8.5 %collective-permute-start.15 = (bf16[1216,512]{1,0:T(8,128)(2,1)}, bf16[1216,512]{1,0:T(8,128)(2,1)S(1)}, u32[]{:S(2)}, u32[]{:S(2)}) collective-permute-start(bf16[1216,512]{1,0:T(8,128)(2,1)} %get-tuple-element.104), channel_id=1, source_target_pairs={{0,4},{4,0},{1,5},{5,1},{2,6},{6,2},{3,7},{7,3},{8,12},{12,8},{9,1... | collective-permute-start | bytes 3735560 | tf_op jit(solution)/shard_map/ppermute | solution.py:851
  101.3 1.2 copy-start.3
  102.9 8.8 %collective-permute-start.14 = (bf16[1024,128]{1,0:T(8,128)(2,1)S(1)}, bf16[1024,128]{1,0:T(8,128)(2,1)S(1)}, u32[]{:S(2)}, u32[]{:S(2)}) collective-permute-start(bf16[1024,128]{1,0:T(8,128)(2,1)S(1)} %get-tuple-element.103), channel_id=1, source_target_pairs={{0,1},{1,2},{2,3},{3,0},{4,5},{5,6},{6,7},{7,4},{8,9},{9,10},{10,1... | collective-permute-start | bytes 786440 | tf_op jit(solution)/shard_map/ppermute | solution.py:857
  104.0 13.9 %collective-permute-start.19 = (bf16[1024,128]{1,0:T(8,128)(2,1)S(1)}, bf16[1024,128]{1,0:T(8,128)(2,1)S(1)}, u32[]{:S(2)}, u32[]{:S(2)}) collective-permute-start(bf16[1024,128]{1,0:T(8,128)(2,1)S(1)} %get-tuple-element.117), channel_id=1, source_target_pairs={{0,2},{1,3},{2,0},{3,1},{4,6},{5,7},{6,4},{7,5},{8,10},{9,11},{10,... | collective-permute-start | bytes 786440 | tf_op jit(solution)/shard_map/ppermute | solution.py:857
  106.1 11.8 %collective-permute-start.20 = (bf16[1024,128]{1,0:T(8,128)(2,1)S(1)}, bf16[1024,128]{1,0:T(8,128)(2,1)S(1)}, u32[]{:S(2)}, u32[]{:S(2)}) collective-permute-start(bf16[1024,128]{1,0:T(8,128)(2,1)S(1)} %get-tuple-element.118), channel_id=1, source_target_pairs={{0,3},{1,0},{2,1},{3,2},{4,7},{5,4},{6,5},{7,6},{8,11},{9,8},{10,9... | collective-permute-start | bytes 786440 | tf_op jit(solution)/shard_map/ppermute | solution.py:857
  112.0 25.8 %collective-permute-start.16 = (bf16[256,512]{1,0:T(8,128)(2,1)S(1)}, bf16[256,512]{1,0:T(8,128)(2,1)S(1)}, u32[]{:S(2)}, u32[]{:S(2)}) collective-permute-start(bf16[256,512]{1,0:T(8,128)(2,1)S(1)} %get-tuple-element.107), channel_id=1, source_target_pairs={{0,24},{8,0},{16,8},{24,16},{1,25},{9,1},{17,9},{25,17},{2,26},{10... | collective-permute-start | bytes 786440 | tf_op jit(solution)/shard_map/ppermute | solution.py:908
  114.6 24.3 %collective-permute-start.17 = (bf16[256,512]{1,0:T(8,128)(2,1)S(1)}, bf16[256,512]{1,0:T(8,128)(2,1)S(1)}, u32[]{:S(2)}, u32[]{:S(2)}) collective-permute-start(bf16[256,512]{1,0:T(8,128)(2,1)S(1)} %get-tuple-element.108), channel_id=1, source_target_pairs={{0,16},{8,24},{16,0},{24,8},{1,17},{9,25},{17,1},{25,9},{2,18},{10... | collective-permute-start | bytes 786440 | tf_op jit(solution)/shard_map/ppermute | solution.py:908
  115.2 23.7 %collective-permute-start.18 = (bf16[256,512]{1,0:T(8,128)(2,1)S(1)}, bf16[256,512]{1,0:T(8,128)(2,1)S(1)}, u32[]{:S(2)}, u32[]{:S(2)}) collective-permute-start(bf16[256,512]{1,0:T(8,128)(2,1)S(1)} %get-tuple-element.109), channel_id=1, source_target_pairs={{0,8},{8,16},{16,24},{24,0},{1,9},{9,17},{17,25},{25,1},{2,10},{10... | collective-permute-start | bytes 786440 | tf_op jit(solution)/shard_map/ppermute | solution.py:908
  123.8 18.3 %all-to-all-start.1 = ((bf16[16,160,128]{2,1,0:T(8,128)(2,1)}), bf16[16,160,128]{2,1,0:T(8,128)(2,1)}, u32[]{:S(2)}, u32[]{:S(2)}) async-start(bf16[16,160,128]{2,1,0:T(8,128)(2,1)} %get-tuple-element.120), calls=%async_computation.1 | async-start | bytes 1310720 | tf_op jit(solution)/shard_map/all_to_all | solution.py:912
  133.9 6.1 %collective-permute-start.21 = (bf16[192,128]{1,0:T(8,128)(2,1)}, bf16[192,128]{1,0:T(8,128)(2,1)}, u32[]{:S(2)}, u32[]{:S(2)}) collective-permute-start(bf16[192,128]{1,0:T(8,128)(2,1)} %copy-done.21), channel_id=1, source_target_pairs={{0,1},{1,2},{2,3},{3,0},{4,5},{5,6},{6,7},{7,4},{8,9},{9,10},{10,1... | collective-permute-start | bytes 147464 | tf_op jit(solution)/shard_map/ppermute | solution.py:857
  135.2 4.9 %collective-permute-start.22 = (bf16[192,128]{1,0:T(8,128)(2,1)}, bf16[192,128]{1,0:T(8,128)(2,1)}, u32[]{:S(2)}, u32[]{:S(2)}) collective-permute-start(bf16[192,128]{1,0:T(8,128)(2,1)} %copy-done.20), channel_id=1, source_target_pairs={{0,2},{1,3},{2,0},{3,1},{4,6},{5,7},{6,4},{7,5},{8,10},{9,11},{10,... | collective-permute-start | bytes 147464 | tf_op jit(solution)/shard_map/ppermute | solution.py:857
  137.8 3.6 %collective-permute-start.23 = (bf16[192,128]{1,0:T(8,128)(2,1)}, bf16[192,128]{1,0:T(8,128)(2,1)}, u32[]{:S(2)}, u32[]{:S(2)}) collective-permute-start(bf16[192,128]{1,0:T(8,128)(2,1)} %copy-done.19), channel_id=1, source_target_pairs={{0,3},{1,0},{2,1},{3,2},{4,7},{5,4},{6,5},{7,6},{8,11},{9,8},{10,9... | collective-permute-start | bytes 147464 | tf_op jit(solution)/shard_map/ppermute | solution.py:857
  140.0 19.5 %copy-start.18 = (bf16[192,512]{1,0:T(8,128)(2,1)}, bf16[192,512]{1,0:T(8,128)(2,1)S(1)}, u32[]{:S(2)}) copy-start(bf16[192,512]{1,0:T(8,128)(2,1)S(1)} %get-tuple-element.132) | copy-start | bytes 589828
  144.3 15.2 %all-to-all-start.2 = ((bf16[16,192,128]{2,1,0:T(8,128)(2,1)}), bf16[16,192,128]{2,1,0:T(8,128)(2,1)S(1)}, u32[]{:S(2)}, u32[]{:S(2)}) async-start(bf16[16,192,128]{2,1,0:T(8,128)(2,1)} %get-tuple-element.128), calls=%async_computation.2 | async-start | bytes 1572864 | tf_op jit(solution)/shard_map/all_to_all | solution.py:916
  150.4 3.8 %collective-permute-start.26 = (bf16[160,128]{1,0:T(8,128)(2,1)S(1)}, bf16[160,128]{1,0:T(8,128)(2,1)S(1)}, u32[]{:S(2)}, u32[]{:S(2)}) collective-permute-start(bf16[160,128]{1,0:T(8,128)(2,1)S(1)} %get-tuple-element.129.d0), channel_id=1, source_target_pairs={{0,3},{1,0},{2,1},{3,2},{4,7},{5,4},{6,5},{7,6},{8,11},{9,8},{10,9... | collective-permute-start | bytes 122888 | tf_op jit(solution)/shard_map/ppermute | solution.py:857
  153.1 4.5 %collective-permute-start.25 = (bf16[160,128]{1,0:T(8,128)(2,1)S(1)}, bf16[160,128]{1,0:T(8,128)(2,1)S(1)}, u32[]{:S(2)}, u32[]{:S(2)}) collective-permute-start(bf16[160,128]{1,0:T(8,128)(2,1)S(1)} %get-tuple-element.129.d0), channel_id=1, source_target_pairs={{0,2},{1,3},{2,0},{3,1},{4,6},{5,7},{6,4},{7,5},{8,10},{9,11},{10,... | collective-permute-start | bytes 122888 | tf_op jit(solution)/shard_map/ppermute | solution.py:857
  153.4 4.5 %collective-permute-start.24 = (bf16[160,128]{1,0:T(8,128)(2,1)S(1)}, bf16[160,128]{1,0:T(8,128)(2,1)S(1)}, u32[]{:S(2)}, u32[]{:S(2)}) collective-permute-start(bf16[160,128]{1,0:T(8,128)(2,1)S(1)} %get-tuple-element.129.d0), channel_id=1, source_target_pairs={{0,1},{1,2},{2,3},{3,0},{4,5},{5,6},{6,7},{7,4},{8,9},{9,10},{10,1... | collective-permute-start | bytes 122888 | tf_op jit(solution)/shard_map/ppermute | solution.py:857
  159.6 53.4 %copy-start.16 = (f32[640]{0:T(1024)S(1)}, f32[640]{0:T(1024)}, u32[]{:S(2)}) copy-start(f32[640]{0:T(1024)} %ga.5) | copy-start | bytes 7684
  159.6 53.3 %copy-start.17 = (s32[1,2]{1,0:T(1,128)S(1)}, s32[1,2]{1,0:T(1,128)}, u32[]{:S(2)}) copy-start(s32[1,2]{1,0:T(1,128)} %lengths.3) | copy-start | bytes 28
  159.6 46.2 %all-to-all-start.3 = ((bf16[16,4,160,128]{3,2,1,0:T(8,128)(2,1)}), bf16[16,4,160,128]{3,2,1,0:T(8,128)(2,1)S(1)}, u32[]{:S(2)}, u32[]{:S(2)}) async-start(bf16[16,4,160,128]{3,2,1,0:T(8,128)(2,1)} %spread.1), calls=%async_computation.3 | async-start | bytes 5242880 | tf_op jit(solution)/shard_map/all_to_all | solution.py:920
  166.6 37.5 %collective-permute-start.29 = (bf16[16,192,128]{2,1,0:T(8,128)(2,1)S(1)}, bf16[16,192,128]{2,1,0:T(8,128)(2,1)S(1)}, u32[]{:S(2)}, u32[]{:S(2)}) collective-permute-start(bf16[16,192,128]{2,1,0:T(8,128)(2,1)S(1)} %all-to-all-done.2.e0_h), channel_id=1, source_target_pairs={{0,3},{1,0},{2,1},{3,2},{4,7},{5,4},{6,5},{7,6},{8,11},{9,8},{10,9... | collective-permute-start | bytes 2359304 | tf_op jit(solution)/shard_map/ppermute | solution.py:857
  167.3 36.8 %collective-permute-start.28 = (bf16[16,192,128]{2,1,0:T(8,128)(2,1)S(1)}, bf16[16,192,128]{2,1,0:T(8,128)(2,1)S(1)}, u32[]{:S(2)}, u32[]{:S(2)}) collective-permute-start(bf16[16,192,128]{2,1,0:T(8,128)(2,1)S(1)} %all-to-all-done.2.e0_h), channel_id=1, source_target_pairs={{0,2},{1,3},{2,0},{3,1},{4,6},{5,7},{6,4},{7,5},{8,10},{9,11},{10,... | collective-permute-start | bytes 2359304 | tf_op jit(solution)/shard_map/ppermute | solution.py:857
  167.8 38.0 %collective-permute-start.27 = (bf16[16,192,128]{2,1,0:T(8,128)(2,1)S(1)}, bf16[16,192,128]{2,1,0:T(8,128)(2,1)}, u32[]{:S(2)}, u32[]{:S(2)}) collective-permute-start(bf16[16,192,128]{2,1,0:T(8,128)(2,1)S(1)} %all-to-all-done.2.e0_h), channel_id=1, source_target_pairs={{0,1},{1,2},{2,3},{3,0},{4,5},{5,6},{6,7},{7,4},{8,9},{9,10},{10,1... | collective-permute-start | bytes 2359304 | tf_op jit(solution)/shard_map/ppermute | solution.py:857
  168.6 34.8 %collective-permute-start.30 = (bf16[192,512]{1,0:T(8,128)(2,1)}, bf16[192,512]{1,0:T(8,128)(2,1)S(1)}, u32[]{:S(2)}, u32[]{:S(2)}) collective-permute-start(bf16[192,512]{1,0:T(8,128)(2,1)} %copy-done.18), channel_id=1, source_target_pairs={{32,0},{64,32},{96,64},{33,1},{65,33},{97,65},{34,2},{66,34},{98,6... | collective-permute-start | bytes 589832 | tf_op jit(solution)/shard_map/ppermute | solution.py:922
  170.7 32.7 %collective-permute-start.31 = (bf16[64,512]{1,0:T(8,128)(2,1)S(1)}, bf16[64,512]{1,0:T(8,128)(2,1)S(1)}, u32[]{:S(2)}, u32[]{:S(2)}) collective-permute-start(bf16[64,512]{1,0:T(8,128)(2,1)S(1)} %get-tuple-element.133), channel_id=1, source_target_pairs={{64,0},{96,32},{65,1},{97,33},{66,2},{98,34},{67,3},{99,35},{68,4}... | collective-permute-start | bytes 196616 | tf_op jit(solution)/shard_map/ppermute | solution.py:923
  205.8 16.4 %collective-permute-start.36 = (bf16[16,4,160,128]{3,2,1,0:T(8,128)(2,1)S(1)}, bf16[16,4,160,128]{3,2,1,0:T(8,128)(2,1)S(1)}, u32[]{:S(2)}, u32[]{:S(2)}) collective-permute-start(bf16[16,4,160,128]{3,2,1,0:T(8,128)(2,1)S(1)} %all-to-all-done.3.f_h), channel_id=1, source_target_pairs={{0,4},{4,0},{1,5},{5,1},{2,6},{6,2},{3,7},{7,3},{8,12},{12,8},{9,1... | collective-permute-start | bytes 7864328 | tf_op jit(solution)/shard_map/ppermute | solution.py:851
  211.9 10.2 %collective-permute-start.32 = (bf16[16,192,128]{2,1,0:T(8,128)(2,1)S(1)}, bf16[16,192,128]{2,1,0:T(8,128)(2,1)S(1)}, u32[]{:S(2)}, u32[]{:S(2)}) collective-permute-start(bf16[16,192,128]{2,1,0:T(8,128)(2,1)S(1)} %all-to-all-done.2.e0_h), channel_id=1, source_target_pairs={{0,4},{4,0},{1,5},{5,1},{2,6},{6,2},{3,7},{7,3},{8,12},{12,8},{9,1... | collective-permute-start | bytes 2359304 | tf_op jit(solution)/shard_map/ppermute | solution.py:851
  212.0 10.2 %collective-permute-start.33 = (bf16[16,192,128]{2,1,0:T(8,128)(2,1)}, bf16[16,192,128]{2,1,0:T(8,128)(2,1)S(1)}, u32[]{:S(2)}, u32[]{:S(2)}) collective-permute-start(bf16[16,192,128]{2,1,0:T(8,128)(2,1)} %collective-permute-done.27.e1_h), channel_id=1, source_target_pairs={{0,4},{4,0},{1,5},{5,1},{2,6},{6,2},{3,7},{7,3},{8,12},{12,8},{9,1... | collective-permute-start | bytes 2359304 | tf_op jit(solution)/shard_map/ppermute | solution.py:851
  212.4 9.7 %collective-permute-start.34 = (bf16[16,192,128]{2,1,0:T(8,128)(2,1)}, bf16[16,192,128]{2,1,0:T(8,128)(2,1)S(1)}, u32[]{:S(2)}, u32[]{:S(2)}) collective-permute-start(bf16[16,192,128]{2,1,0:T(8,128)(2,1)} %copy-done.6), channel_id=1, source_target_pairs={{0,4},{4,0},{1,5},{5,1},{2,6},{6,2},{3,7},{7,3},{8,12},{12,8},{9,1... | collective-permute-start | bytes 2359304 | tf_op jit(solution)/shard_map/ppermute | solution.py:851
  212.5 9.7 %collective-permute-start.35 = (bf16[16,192,128]{2,1,0:T(8,128)(2,1)}, bf16[16,192,128]{2,1,0:T(8,128)(2,1)S(1)}, u32[]{:S(2)}, u32[]{:S(2)}) collective-permute-start(bf16[16,192,128]{2,1,0:T(8,128)(2,1)} %copy-done.4), channel_id=1, source_target_pairs={{0,4},{4,0},{1,5},{5,1},{2,6},{6,2},{3,7},{7,3},{8,12},{12,8},{9,1... | collective-permute-start | bytes 2359304 | tf_op jit(solution)/shard_map/ppermute | solution.py:851
  212.9 0.9 copy-start.1
  213.9 1.0 copy-start.8
  214.9 1.0 copy-start.9
  215.9 1.0 copy-start.11
  216.9 1.0 copy-start.12
  217.9 1.0 copy-start.13
  218.9 0.9 copy-start.15
  219.8 2.4 %copy-start.5 = (bf16[16,192,128]{2,1,0:T(8,128)(2,1)S(1)}, bf16[16,192,128]{2,1,0:T(8,128)(2,1)}, u32[]{:S(2)}) copy-start(bf16[16,192,128]{2,1,0:T(8,128)(2,1)} %copy-done.4) | copy-start | bytes 2359300
  219.8 2.4 %copy-start.7 = (bf16[16,192,128]{2,1,0:T(8,128)(2,1)S(1)}, bf16[16,192,128]{2,1,0:T(8,128)(2,1)}, u32[]{:S(2)}) copy-start(bf16[16,192,128]{2,1,0:T(8,128)(2,1)} %copy-done.6) | copy-start | bytes 2359300
  (9 other events, 6.5 us)
